TPU v7x, 32 devices: a whole 2x2x4 slice. The times are simulated.
32 devices in a mesh: dp: 8 (over z, x), row: 4 (over y, core).
Axes of the slice: x: 2, y: 2, z: 4, core: 2. Of those that a mesh axis runs over, the one named last changes fastest.
Arguments:
- image: bfloat16 [2, 64, 28, 28, 256], P(None, 'dp', 'row'), may hold values from -6 to 6
- tags: bfloat16 [2, 64, 128, 512], P(None, ('dp', 'row')), may hold values from -6 to 6
- tag_lengths: int32 [2, 64], P(None, ('dp', 'row')), may hold values from 40 to 128, as said below
- cotangent: bfloat16 [2, 64, 128, 512], P(None, ('dp', 'row')), may hold values from -6 to 6
- conv_weight: bfloat16 [2, 3, 3, 256, 256], replicated, may hold values from -0.125 to 0.125
- bn_mean: float32 [2, 256], replicated, may hold values from -3 to 3
- bn_var: float32 [2, 256], replicated, may hold values from 0.25 to 4
- bn_scale: float32 [2, 256], replicated, may hold values from 0.25 to 1.75
- bn_shift: float32 [2, 256], replicated, may hold values from -3 to 3
- proj_weight: bfloat16 [256, 512], replicated, may hold values from -0.375 to 0.375
- proj_bias: float32 [512], replicated, may hold values from -3 to 3
- attn_in: bfloat16 [6, 512, 512], replicated, may hold values from -0.25 to 0.25
- attn_out: bfloat16 [2, 512, 512], replicated, may hold values from -1 to 1
- ln_gain: float32 [3, 512], replicated, may hold values from 0.25 to 1.75
- ln_bias: float32 [3, 512], replicated, may hold values from -3 to 3
- ffn_in: bfloat16 [512, 1024], replicated, may hold values from -0.25 to 0.25
- ffn_in_bias: float32 [1024], replicated, may hold values from -3 to 3
- ffn_out: bfloat16 [1024, 512], replicated, may hold values from -0.1875 to 0.1875
- ffn_out_bias: float32 [512], replicated, may hold values from -3 to 3
Outputs:
- decoded: bfloat16 [2, 64, 128, 512], P(None, ('dp', 'row'))
- image_grad: float32 [2, 64, 28, 28, 256], P(None, 'dp', 'row')
- tags_grad: float32 [2, 64, 128, 512], P(None, ('dp', 'row'))
- conv_grad: float32 [2, 3, 3, 256, 256], replicated
- bn_scale_grad: float32 [2, 256], replicated
- bn_shift_grad: float32 [2, 256], replicated
- proj_grad: float32 [256, 512], replicated
- proj_bias_grad: float32 [512], replicated
- attn_in_grad: float32 [6, 512, 512], replicated
- attn_out_grad: float32 [2, 512, 512], replicated
- ln_gain_grad: float32 [3, 512], replicated
- ln_bias_grad: float32 [3, 512], replicated
- ffn_in_grad: float32 [512, 1024], replicated
- ffn_in_bias_grad: float32 [1024], replicated
- ffn_out_grad: float32 [1024, 512], replicated
- ffn_out_bias_grad: float32 [512], replicated
Inputs may be any that keep to these rules, and one draw needn't show every extreme that they name: `tag_lengths`: slot j of a table holds a tag when j is below its count; in every micro-batch some table has exactly 128.
All inputs are finite; a program needn't handle non-finite values.
Results may differ from a plain program's by a relative error of at most 0.023.
Values may be sent and summed in bfloat16 or wider, within the bound.
A program may use at most 256 MiB of HBM per device.

v0:
```python
import math

import jax
import jax.numpy as jnp
from jax import lax
from jax.sharding import PartitionSpec as P

HEADS = 8


EPS = 1e-05
MASKED = -1e30


def padded_2(value, sides, width):
    for axis, dim in sides:
        size, length = (lax.axis_size(axis), value.shape[dim])
        up = [(i, (i + 1) % size) for i in range(size - 1)]
        down = [(j, i) for i, j in up]
        last = lax.slice_in_dim(value, length - width, length, axis=dim)
        leading = lax.slice_in_dim(value, 0, width, axis=dim)
        before = lax.ppermute(last, axis, up)
        after = lax.ppermute(leading, axis, down)
        value = jnp.concatenate([before, value, after], axis=dim)
    return value


def layer_norm(inputs, scaling, offset):
    center = inputs - jnp.mean(inputs, -1, keepdims=True)
    spread = jnp.mean(center * center, -1, keepdims=True)
    return center * lax.rsqrt(spread + EPS) * scaling + offset


def smooth(inputs):
    return jax.nn.gelu(inputs, approximate=False)


def smooth_grad(inputs, upstream):
    return jax.vjp(smooth, inputs)[1](upstream)[0]


def norm_grad(inputs, scaling, offset, upstream):
    pullback = jax.vjp(layer_norm, inputs, scaling, offset)[1]
    return pullback(upstream)


def edge_rows(inputs):
    return padded_2(inputs, (("row", 1),), 1)


def edge_grads(inputs):
    return padded_2(inputs, (("row", 1),), 1)


def conv_rows(padded, kernel):
    height = padded.shape[1] - 2
    breadth = padded.shape[2]
    widened = jnp.pad(padded, ((0, 0), (0, 0), (1, 1), (0, 0)))
    summed = jnp.zeros((padded.shape[0], height, breadth, kernel.shape[-1]), jnp.float32)
    for step_a in range(3):
        for step_b in range(3):
            window = widened[:, step_a : step_a + height, step_b : step_b + breadth, :]
            summed = summed + jnp.einsum(
                "grwc,cd->grwd", window, kernel[step_a, step_b], preferred_element_type=jnp.float32
            )
    return summed


def conv_back(padded, kernel):
    height = padded.shape[1] - 2
    breadth = padded.shape[2]
    widened = jnp.pad(padded, ((0, 0), (0, 0), (1, 1), (0, 0)))
    summed = jnp.zeros((padded.shape[0], height, breadth, kernel.shape[-2]), jnp.float32)
    for step_a in range(3):
        for step_b in range(3):
            window = widened[
                :, 2 - step_a : 2 - step_a + height, 2 - step_b : 2 - step_b + breadth, :
            ]
            summed = summed + jnp.einsum(
                "grwd,cd->grwc", window, kernel[step_a, step_b], preferred_element_type=jnp.float32
            )
    return summed


def kernel_grad(padded, upstream):
    height = upstream.shape[1]
    breadth = upstream.shape[2]
    widened = jnp.pad(padded, ((0, 0), (0, 0), (1, 1), (0, 0)))
    pieces = []
    for step_a in range(3):
        for step_b in range(3):
            window = widened[:, step_a : step_a + height, step_b : step_b + breadth, :]
            pieces.append(
                jnp.einsum("grwc,grwd->cd", window, upstream, preferred_element_type=jnp.float32)
            )
    return jnp.stack(pieces).reshape((3, 3) + pieces[0].shape)


def head_view(matrix):
    return matrix.reshape(matrix.shape[0], matrix.shape[1], HEADS, matrix.shape[2] // HEADS)


def scores_of(queries, keys_in, allowed, scale):
    scores = (
        jnp.einsum(
            "oqhe,okhe->ohqk",
            head_view(queries),
            head_view(keys_in),
            preferred_element_type=jnp.float32,
        )
        * scale
    )
    if allowed is None:
        return scores
    return jnp.where(allowed, scores, MASKED)


def attend(queries, keys_in, values_in, allowed, scale):
    scores = scores_of(queries, keys_in, allowed, scale)
    highest = jnp.max(scores, -1, keepdims=True)
    raised = jnp.exp(scores - highest)
    totals = jnp.sum(raised, -1, keepdims=True)
    shares = raised / totals
    logsum = highest + jnp.log(totals)
    mixed = jnp.einsum(
        "ohqk,okhe->oqhe",
        shares.astype(jnp.bfloat16),
        head_view(values_in),
        preferred_element_type=jnp.float32,
    )
    return (mixed.reshape(queries.shape).astype(jnp.bfloat16), logsum)


def attend_back(queries, keys_in, values_in, allowed, scale, logsum, upstream):
    scores = scores_of(queries, keys_in, allowed, scale)
    shares = jnp.exp(scores - logsum)
    up_heads = head_view(upstream)
    grad_shares = jnp.einsum(
        "oqhe,okhe->ohqk", up_heads, head_view(values_in), preferred_element_type=jnp.float32
    )
    grad_scores = (
        shares * (grad_shares - jnp.sum(grad_shares * shares, -1, keepdims=True))
    ).astype(jnp.bfloat16)
    grad_query = (
        jnp.einsum(
            "ohqk,okhe->oqhe", grad_scores, head_view(keys_in), preferred_element_type=jnp.float32
        )
        * scale
    )
    grad_key = (
        jnp.einsum(
            "ohqk,oqhe->okhe", grad_scores, head_view(queries), preferred_element_type=jnp.float32
        )
        * scale
    )
    grad_value = jnp.einsum(
        "ohqk,oqhe->okhe", shares.astype(jnp.bfloat16), up_heads, preferred_element_type=jnp.float32
    )
    return (
        grad_query.reshape(queries.shape),
        grad_key.reshape(keys_in.shape),
        grad_value.reshape(values_in.shape),
    )


def body(
    image,
    tags,
    tag_lengths,
    cotangent,
    conv_weight,
    bn_mean,
    bn_var,
    bn_scale,
    bn_shift,
    proj_weight,
    proj_bias,
    attn_in,
    attn_out,
    ln_gain,
    ln_bias,
    ffn_in,
    ffn_in_bias,
    ffn_out,
    ffn_out_bias,
):
    batches = image.shape[0]
    owned = tags.shape[1]
    slots = tags.shape[2]
    scale = 1.0 / math.sqrt(tags.shape[3] // HEADS)
    factor = lax.rsqrt(bn_var + EPS)
    position = jnp.arange(slots)
    causal = (position[None, :] <= position[:, None])[None, None]
    decoded = []
    image_grad = []
    tags_grad = []
    running = None
    for batch in range(batches):
        inputs = image[batch]
        padded_in = edge_rows(inputs)
        pre_one = conv_rows(padded_in, conv_weight[0])
        norm_one = (pre_one - bn_mean[0]) * factor[0]
        act_one = norm_one * bn_scale[0] + bn_shift[0]
        hidden = smooth(act_one).astype(jnp.bfloat16)
        padded_mid = edge_rows(hidden)
        pre_two = conv_rows(padded_mid, conv_weight[1])
        norm_two = (pre_two - bn_mean[1]) * factor[1]
        act_two = norm_two * bn_scale[1] + bn_shift[1] + inputs.astype(jnp.float32)
        block_out = smooth(act_two).astype(jnp.bfloat16)
        tokens = (
            jnp.einsum("grwc,cd->grwd", block_out, proj_weight, preferred_element_type=jnp.float32)
            + proj_bias
        ).astype(jnp.bfloat16)
        every = lax.all_gather(tokens, "row", axis=1, tiled=True)
        mine = lax.dynamic_slice_in_dim(every, lax.axis_index("row") * owned, owned, 0)
        memory = mine.reshape(owned, mine.shape[1] * mine.shape[2], mine.shape[3])
        start = tags[batch]
        lengths = tag_lengths[batch]
        allowed = causal & (position[None, :] < lengths[:, None])[:, None, None, :]
        projected = jnp.einsum(
            "old,jde->jole", start, attn_in[:3], preferred_element_type=jnp.float32
        ).astype(jnp.bfloat16)
        self_mix, self_log = attend(projected[0], projected[1], projected[2], allowed, scale)
        first_in = start.astype(jnp.float32) + jnp.einsum(
            "old,de->ole", self_mix, attn_out[0], preferred_element_type=jnp.float32
        )
        first = layer_norm(first_in, ln_gain[0], ln_bias[0])
        first_b = first.astype(jnp.bfloat16)
        cross_q = jnp.einsum(
            "old,de->ole", first_b, attn_in[3], preferred_element_type=jnp.float32
        ).astype(jnp.bfloat16)
        cross_kv = jnp.einsum(
            "oid,jde->joie", memory, attn_in[4:6], preferred_element_type=jnp.float32
        ).astype(jnp.bfloat16)
        cross_mix, cross_log = attend(cross_q, cross_kv[0], cross_kv[1], None, scale)
        second_in = first + jnp.einsum(
            "old,de->ole", cross_mix, attn_out[1], preferred_element_type=jnp.float32
        )
        second = layer_norm(second_in, ln_gain[1], ln_bias[1])
        second_b = second.astype(jnp.bfloat16)
        inner = (
            jnp.einsum("old,df->olf", second_b, ffn_in, preferred_element_type=jnp.float32)
            + ffn_in_bias
        )
        inner_act = smooth(inner).astype(jnp.bfloat16)
        third_in = (
            second
            + jnp.einsum("olf,fd->old", inner_act, ffn_out, preferred_element_type=jnp.float32)
            + ffn_out_bias
        )
        decoded.append(layer_norm(third_in, ln_gain[2], ln_bias[2]).astype(jnp.bfloat16))
        grad_third, gain_three, shift_three = norm_grad(
            third_in, ln_gain[2], ln_bias[2], cotangent[batch].astype(jnp.float32)
        )
        grad_outer = grad_third.astype(jnp.bfloat16)
        ffn_out_g = jnp.einsum(
            "olf,old->fd", inner_act, grad_outer, preferred_element_type=jnp.float32
        )
        ffn_out_bias_g = jnp.sum(grad_outer.astype(jnp.float32), axis=(0, 1))
        grad_act = jnp.einsum(
            "old,fd->olf", grad_outer, ffn_out, preferred_element_type=jnp.float32
        )
        grad_inner = smooth_grad(inner, grad_act).astype(jnp.bfloat16)
        ffn_in_g = jnp.einsum(
            "old,olf->df", second_b, grad_inner, preferred_element_type=jnp.float32
        )
        ffn_in_bias_g = jnp.sum(grad_inner.astype(jnp.float32), axis=(0, 1))
        grad_second = grad_third + jnp.einsum(
            "olf,df->old", grad_inner, ffn_in, preferred_element_type=jnp.float32
        )
        grad_second_in, gain_two, shift_two = norm_grad(
            second_in, ln_gain[1], ln_bias[1], grad_second
        )
        grad_cross_out = grad_second_in.astype(jnp.bfloat16)
        out_two_g = jnp.einsum(
            "old,ole->de", cross_mix, grad_cross_out, preferred_element_type=jnp.float32
        )
        grad_cross_mix = jnp.einsum(
            "ole,de->old", grad_cross_out, attn_out[1], preferred_element_type=jnp.float32
        ).astype(jnp.bfloat16)
        cross_grads = attend_back(
            cross_q, cross_kv[0], cross_kv[1], None, scale, cross_log, grad_cross_mix
        )
        grad_cross_q = cross_grads[0].astype(jnp.bfloat16)
        grad_cross_kv = jnp.stack([cross_grads[1], cross_grads[2]]).astype(jnp.bfloat16)
        in_three_g = jnp.einsum(
            "old,ole->de", first_b, grad_cross_q, preferred_element_type=jnp.float32
        )
        in_pair_g = jnp.einsum(
            "oid,joie->jde", memory, grad_cross_kv, preferred_element_type=jnp.float32
        )
        grad_memory = jnp.einsum(
            "joie,jde->oid", grad_cross_kv, attn_in[4:6], preferred_element_type=jnp.float32
        )
        grad_first = grad_second_in + jnp.einsum(
            "ole,de->old", grad_cross_q, attn_in[3], preferred_element_type=jnp.float32
        )
        grad_first_in, gain_one, shift_one = norm_grad(first_in, ln_gain[0], ln_bias[0], grad_first)
        grad_self_out = grad_first_in.astype(jnp.bfloat16)
        out_one_g = jnp.einsum(
            "old,ole->de", self_mix, grad_self_out, preferred_element_type=jnp.float32
        )
        grad_self_mix = jnp.einsum(
            "ole,de->old", grad_self_out, attn_out[0], preferred_element_type=jnp.float32
        ).astype(jnp.bfloat16)
        self_grads = attend_back(
            projected[0], projected[1], projected[2], allowed, scale, self_log, grad_self_mix
        )
        grad_projected = jnp.stack([self_grads[0], self_grads[1], self_grads[2]]).astype(
            jnp.bfloat16
        )
        in_self_g = jnp.einsum(
            "old,jole->jde", start, grad_projected, preferred_element_type=jnp.float32
        )
        tags_grad.append(
            grad_first_in
            + jnp.einsum(
                "jole,jde->old", grad_projected, attn_in[:3], preferred_element_type=jnp.float32
            )
        )
        grad_mine = grad_memory.reshape(mine.shape)
        placed = lax.dynamic_update_slice_in_dim(
            jnp.zeros(every.shape, jnp.float32), grad_mine, lax.axis_index("row") * owned, 0
        )
        grad_tokens = lax.psum_scatter(
            placed.astype(jnp.bfloat16), "row", scatter_dimension=1, tiled=True
        )
        proj_g = jnp.einsum(
            "grwc,grwd->cd", block_out, grad_tokens, preferred_element_type=jnp.float32
        )
        proj_bias_g = jnp.sum(grad_tokens.astype(jnp.float32), axis=(0, 1, 2))
        grad_block = jnp.einsum(
            "grwd,cd->grwc", grad_tokens, proj_weight, preferred_element_type=jnp.float32
        )
        grad_act_two = smooth_grad(act_two, grad_block)
        scale_two_g = jnp.sum(grad_act_two * norm_two, axis=(0, 1, 2))
        shift_two_g = jnp.sum(grad_act_two, axis=(0, 1, 2))
        grad_pre_two = (grad_act_two * bn_scale[1] * factor[1]).astype(jnp.bfloat16)
        conv_two_g = kernel_grad(padded_mid, grad_pre_two)
        grad_hidden = conv_back(edge_grads(grad_pre_two), conv_weight[1])
        grad_act_one = smooth_grad(act_one, grad_hidden)
        scale_one_g = jnp.sum(grad_act_one * norm_one, axis=(0, 1, 2))
        shift_one_g = jnp.sum(grad_act_one, axis=(0, 1, 2))
        grad_pre_one = (grad_act_one * bn_scale[0] * factor[0]).astype(jnp.bfloat16)
        conv_one_g = kernel_grad(padded_in, grad_pre_one)
        image_grad.append(conv_back(edge_grads(grad_pre_one), conv_weight[0]) + grad_act_two)
        local = (
            jnp.stack([conv_one_g, conv_two_g]),
            jnp.stack([scale_one_g, scale_two_g]),
            jnp.stack([shift_one_g, shift_two_g]),
            proj_g,
            proj_bias_g,
            jnp.concatenate([in_self_g, in_three_g[None], in_pair_g]),
            jnp.stack([out_one_g, out_two_g]),
            jnp.stack([gain_one, gain_two, gain_three]),
            jnp.stack([shift_one, shift_two, shift_three]),
            ffn_in_g,
            ffn_in_bias_g,
            ffn_out_g,
            ffn_out_bias_g,
        )
        running = local if running is None else jax.tree.map(jnp.add, running, local)
    summed = lax.psum(
        (
            running[0],
            running[1],
            running[2],
            running[3],
            running[4],
            running[5],
            running[6],
            running[7],
            running[8],
            running[9],
            running[10],
            running[11],
            running[12],
        ),
        ("dp", "row"),
    )
    return (
        jnp.stack(decoded),
        jnp.stack(image_grad),
        jnp.stack(tags_grad),
        summed[0],
        summed[1],
        summed[2],
        summed[3],
        summed[4],
        summed[5],
        summed[6],
        summed[7],
        summed[8],
        summed[9],
        summed[10],
        summed[11],
        summed[12],
    )


def solution(mesh):
    placed = (
        P(None, "dp", "row", None, None),
        P(None, ("dp", "row"), None, None),
        P(None, ("dp", "row")),
        P(None, ("dp", "row"), None, None),
        P(),
        P(),
        P(),
        P(),
        P(),
        P(),
        P(),
        P(),
        P(),
        P(),
        P(),
        P(),
        P(),
        P(),
        P(),
    )
    return jax.shard_map(
        body,
        mesh=mesh,
        in_specs=placed,
        out_specs=(
            P(None, ("dp", "row"), None, None),
            P(None, "dp", "row", None, None),
            P(None, ("dp", "row"), None, None),
            P(),
            P(),
            P(),
            P(),
            P(),
            P(),
            P(),
            P(),
            P(),
            P(),
            P(),
            P(),
            P(),
        ),
        check_vma=False,
    )
```

profile of v0, /device:TPU:1, one launch (start us, length us, event | category | flops | bytes accessed | tf_op | source)
XLA Modules:
  0.0 808.2 jit_solution(6645448568796561132)
XLA Ops:
  9.1 4.8 collective-permute-start.4
  16.1 3.6 collective-permute-start
  32.2 10.6 %multiply_convert_fusion.11 = (bf16[8,7,28,256]{3,2,1,0:T(8,128)(2,1)S(1)}, bf16[8,7,28,256]{3,2,1,0:T(8,128)(2,1)S(1)}, f32[8,7,28,256]{3,2,1,0:T(8,128)}) fusion(f32[256]{0:T(256)S(1)} %bitcast.1166, f32[256]{0:T(256)S(1)} %bitcast.1163, f32[8,7,28,256]{3,2,1,0:T(8,128)S(1)} %subtract_multiply_fusion.1, f32[256]{0:T(256)S(1)} %bitcast.1148, ...), kind=kOutput, calls=%fused_computation.118 | convolution fusion | flops 263323648 | bytes 20779008 | tf_op jit(solution)/shard_map/grwc,cd->grwd/dot_general | solution.py:63
  42.8 3.6 collective-permute-start.2
  49.2 3.6 collective-permute-start.6
  52.8 2.4 collective-permute-start.7
  65.7 11.1 %multiply_convert_fusion.10 = (bf16[8,7,28,256]{3,2,1,0:T(8,128)(2,1)S(1)}, f32[8,7,28,256]{3,2,1,0:T(8,128)}, bf16[8,7,28,256]{3,2,1,0:T(8,128)(2,1)}, f32[8,7,28,256]{3,2,1,0:T(8,128)}, f32[8,7,28,256]{3,2,1,0:T(8,128)}) fusion(f32[256]{0:T(256)S(1)} %bitcast.1172, f32[256]{0:T(256)S(1)} %bitcast.1169, ...), kind=kOutput, calls=%fused_computation.103 | convolution fusion | flops 264929280 | bytes 25595904 | tf_op jit(solution)/shard_map/grwc,cd->grwd/dot_general | solution.py:63
  91.2 2.2 fusion.88
  95.9 2.1 convolution_convert_fusion.8
  99.2 33.2 %all-gather.3.cloned.1.call-done = bf16[8,28,28,512]{3,2,1,0:T(8,128)(2,1)} async-done(((bf16[8,7,28,512]{3,2,1,0:T(8,128)(2,1)}), bf16[8,28,28,512]{3,2,1,0:T(8,128)(2,1)}) %all-gather.3.cloned.1.call-update) | async-done | bytes 6422544 | tf_op jit(solution)/shard_map/all_gather | solution.py:214
  132.4 54.5 %all-gather.5.cloned.1.call-done = bf16[8,28,28,512]{3,2,1,0:T(8,128)(2,1)} async-done(((bf16[8,7,28,512]{3,2,1,0:T(8,128)(2,1)}), bf16[8,28,28,512]{3,2,1,0:T(8,128)(2,1)}) %all-gather.5.cloned.1.call-update) | async-done | bytes 6422544 | tf_op jit(solution)/shard_map/all_gather | solution.py:214
  186.9 3.7 constant_dynamic-slice_fusion
  192.2 3.6 convert_bitcast_fusion
  197.9 3.7 copy.186
  201.5 3.3 copy.184
  204.8 2.8 multiply_reduce_fusion.2
  214.1 3.2 multiply_convert_fusion.14
  220.9 3.6 convert_bitcast_fusion.1
  226.5 3.3 copy.177
  229.8 3.4 copy.175
  233.2 2.7 multiply_reduce_fusion.3
  242.0 2.4 multiply_convert_fusion.15
  258.8 5.5 multiply_reduce_fusion
  264.3 2.6 fusion.48
  268.6 2.4 multiply_convert_fusion.2
  271.0 3.6 copy.194
  274.6 2.7 copy.195
  277.3 4.1 fusion.20
  283.0 3.4 broadcast.551.clone
  286.4 2.4 constant_dynamic-update-slice_fusion
  292.0 5.5 multiply_reduce_fusion.1
  300.0 2.4 multiply_convert_fusion.3
  302.4 3.5 copy.189
  305.9 4.2 fusion.45
  310.1 2.3 copy.190
  312.4 4.1 fusion.19
  318.1 3.4 broadcast.551.clone.1
  321.5 2.4 constant_dynamic-update-slice_fusion.1
  325.7 2.9 fusion.125
  331.9 2.4 multiply_reduce_fusion.13
  349.5 2.2 fusion.121
  368.5 2.3 bitcast_add_fusion.1
  371.6 2.1 fusion.60
  374.7 2.1 fusion.59
  376.9 3.5 maximum_add_fusion
  380.4 6.5 fusion.511
  390.5 19.2 %reduce-scatter.3.cloned.1.call-done = bf16[8,7,28,512]{3,0,2,1:T(8,128)(2,1)} async-done(((bf16[8,28,28,512]{3,0,2,1:T(8,128)(2,1)}), bf16[8,7,28,512]{3,0,2,1:T(8,128)(2,1)}) %reduce-scatter.3.cloned.1.call-update) | async-done | bytes 1605648 | tf_op jit(solution)/shard_map/reduce_scatter | solution.py:325
  409.6 6.8 fusion.513
  417.4 2.7 collective-permute-start.13
  420.1 3.2 collective-permute-start.12
  439.1 3.6 collective-permute-start.8
  454.5 8.7 %fusion.510 = (f32[256]{0:T(256)}, f32[256]{0:T(256)}, bf16[8,7,28,256]{3,2,1,0:T(8,128)(2,1)S(1)}) fusion(f32[8,7,28,256]{3,2,1,0:T(8,128)S(1)} %copy-done.104, f32[256]{0:T(256)S(1)} %bitcast.1149, f32[256]{0:T(256)S(1)} %bitcast.1164, bf16[3,3,256,256]{3,2,1,0:T(8,128)(2,1)S(1)} %copy-done.22, bf16[8,9,30,256]{3,2,1,0:T(8,128)(2,1)S(1)} %select_maximum_fusion.2, ...), kind=kOutput, calls=%fused_computation.781 | convolution fusion | flops 240442880 | bytes 17454080 | tf_op jit(solution)/shard_map/grwd,cd->grwc/dot_general | solution.py:79
  471.6 6.9 fusion.512
  484.9 2.8 maximum_add_fusion.1
  490.6 2.2 fusion.117
  499.9 3.6 collective-permute-start.10
  506.2 3.6 collective-permute-start.14
  514.4 41.6 %all-reduce.8 = (f32[2,256]{1,0:T(2,128)}, f32[2,256]{1,0:T(2,128)}, f32[512]{0:T(512)}, f32[3,512]{1,0:T(4,128)}, f32[3,512]{1,0:T(4,128)}, /*index=5*/f32[1024]{0:T(1024)}, f32[512]{0:T(512)}) all-reduce(f32[2,256]{1,0:T(2,128)} %maximum_add_fusion.5, ...), channel_id=1, replica_groups=mesh['dp'=8,'row'=4] {'dp','row'}, use_global_device_ids=true, to_apply=%region_43.44 | all-reduce | flops 6144 | bytes 49152 | tf_op jit(solution)/shard_map/psum | solution.py:363
  565.9 3.5 add_bitcast_fusion.1
  569.5 2.7 add_bitcast_fusion
  572.6 4.1 copy.234
  576.6 206.4 %all-reduce.12.cloned.1.call-done = (f32[2,3,3,256,256]{4,3,2,1,0:T(8,128)}, f32[256,512]{1,0:T(8,128)}, f32[6,512,512]{1,2,0:T(8,128)}, f32[2,512,512]{2,1,0:T(...) async-done(((f32[2,3,3,256,256]{4,3,2,1,0:T(8,128)}, f32[256,512]{1,0:T(8,128)}, f32[6,512,512]{1,2,0:T(8,128)}, f32[2,512,512]{2,1,0:T(8,128)}, f32[512,1024]{1,0:T(8,128)}, ...) | async-done | bytes 17825808 | tf_op jit(solution)/shard_map/psum | solution.py:363
  783.0 6.6 copy.235
  789.6 5.1 copy.441
  (874 shorter events, 211.3 us)
Async XLA Ops:
  7.2 206.2 %copy-start = (bf16[512,1024]{1,0:T(8,128)(2,1)S(1)}, bf16[512,1024]{1,0:T(8,128)(2,1)}, u32[]{:S(2)}) copy-start(bf16[512,1024]{1,0:T(8,128)(2,1)} %param.34) | copy-start | bytes 3145732
  7.2 125.2 %all-gather.3.cloned.1.call-start = ((), (), s32[]{:S(2)}) async-start(), calls=%async_computation.2 | async-start | bytes 9175040 | tf_op jit(solution)/shard_map/all_gather | solution.py:214
  8.8 56.5 %copy-start.58 = (bf16[1,8,7,28,256]{4,1,3,2,0:T(8,128)(2,1)}, bf16[1,8,7,28,256]{4,1,3,2,0:T(8,128)(2,1)S(1)}, u32[]{:S(2)}) copy-start(bf16[1,8,7,28,256]{4,1,3,2,0:T(8,128)(2,1)S(1)} %get-tuple-element.143) | copy-start | bytes 2408452
  8.8 56.5 %copy-start.60 = (bf16[1,8,7,28,256]{4,1,3,2,0:T(8,128)(2,1)}, bf16[1,8,7,28,256]{4,1,3,2,0:T(8,128)(2,1)S(1)}, u32[]{:S(2)}) copy-start(bf16[1,8,7,28,256]{4,1,3,2,0:T(8,128)(2,1)S(1)} %get-tuple-element.144) | copy-start | bytes 2408452
  8.8 12.8 %copy-start.81 = (bf16[2,3,3,256,256]{4,3,2,1,0:T(8,128)(2,1)S(1)}, bf16[2,3,3,256,256]{4,3,2,1,0:T(8,128)(2,1)}, u32[]{:S(2)}) copy-start(bf16[2,3,3,256,256]{4,3,2,1,0:T(8,128)(2,1)} %param.23) | copy-start | bytes 7077892
  9.0 20.1 %copy-start.35 = (bf16[1,8,7,28,256]{4,3,2,1,0:T(8,128)(2,1)}, bf16[1,8,7,28,256]{4,3,2,1,0:T(8,128)(2,1)S(1)}, u32[]{:S(2)}) copy-start(bf16[1,8,7,28,256]{4,3,2,1,0:T(8,128)(2,1)S(1)} %copy.399) | copy-start | bytes 2408452
  9.1 14.1 %collective-permute-start.4 = (bf16[8,1,28,256]{3,2,1,0:T(8,128)(2,1)S(1)}, bf16[8,1,28,256]{3,2,1,0:T(8,128)(2,1)S(1)}, u32[]{:S(2)}, u32[]{:S(2)}) collective-permute-start(bf16[8,1,28,256]{3,2,1,0:T(8,128)(2,1)S(1)} %get-tuple-element.159), channel_id=1, source_target_pairs={{0,1},{1,2},{2,3},{4,5},{5,6},{6,7},{8,9},{9,10},{10,11},{12,13},{... | collective-permute-start | bytes 344072 | tf_op jit(solution)/shard_map/ppermute | solution.py:22
  13.9 9.3 %collective-permute-start.5 = (bf16[8,1,28,256]{3,2,1,0:T(8,128)(2,1)S(1)}, bf16[8,1,28,256]{3,2,1,0:T(8,128)(2,1)S(1)}, u32[]{:S(2)}, u32[]{:S(2)}) collective-permute-start(bf16[8,1,28,256]{3,2,1,0:T(8,128)(2,1)S(1)} %get-tuple-element.160), channel_id=1, source_target_pairs={{1,0},{2,1},{3,2},{5,4},{6,5},{7,6},{9,8},{10,9},{11,10},{13,12},{... | collective-permute-start | bytes 344072 | tf_op jit(solution)/shard_map/ppermute | solution.py:23
  16.0 15.3 %copy-start.33 = (bf16[1,8,7,28,256]{4,3,2,1,0:T(8,128)(2,1)}, bf16[1,8,7,28,256]{4,3,2,1,0:T(8,128)(2,1)S(1)}, u32[]{:S(2)}) copy-start(bf16[1,8,7,28,256]{4,3,2,1,0:T(8,128)(2,1)S(1)} %copy.400) | copy-start | bytes 2408452
  16.1 9.9 %collective-permute-start = (bf16[8,1,28,256]{3,2,1,0:T(8,128)(2,1)S(1)}, bf16[8,1,28,256]{3,2,1,0:T(8,128)(2,1)S(1)}, u32[]{:S(2)}, u32[]{:S(2)}) collective-permute-start(bf16[8,1,28,256]{3,2,1,0:T(8,128)(2,1)S(1)} %get-tuple-element.155), channel_id=1, source_target_pairs={{0,1},{1,2},{2,3},{4,5},{5,6},{6,7},{8,9},{9,10},{10,11},{12,13},{... | collective-permute-start | bytes 344072 | tf_op jit(solution)/shard_map/ppermute | solution.py:22
  19.7 6.3 collective-permute-start.1
  21.8 9.9 %copy-start.11 = (bf16[3,3,256,256]{3,2,1,0:T(8,128)(2,1)}, bf16[3,3,256,256]{3,2,1,0:T(8,128)(2,1)S(1)}, u32[]{:S(2)}) copy-start(bf16[3,3,256,256]{3,2,1,0:T(8,128)(2,1)S(1)} %get-tuple-element.138) | copy-start | bytes 3538948
  21.8 43.5 %copy-start.21 = (bf16[3,3,256,256]{3,2,1,0:T(8,128)(2,1)}, bf16[3,3,256,256]{3,2,1,0:T(8,128)(2,1)S(1)}, u32[]{:S(2)}) copy-start(bf16[3,3,256,256]{3,2,1,0:T(8,128)(2,1)S(1)} %get-tuple-element.137) | copy-start | bytes 3538948
  23.0 8.7 %copy-start.242 = (f32[1,256]{1,0:T(1,128)}, f32[1,256]{1,0:T(1,128)S(1)}, u32[]{:S(2)}) copy-start(f32[1,256]{1,0:T(1,128)S(1)} %get-tuple-element.199) | copy-start | bytes 3076
  23.0 42.3 %copy-start.244 = (f32[1,256]{1,0:T(1,128)}, f32[1,256]{1,0:T(1,128)S(1)}, u32[]{:S(2)}) copy-start(f32[1,256]{1,0:T(1,128)S(1)} %get-tuple-element.198) | copy-start | bytes 3076
  23.1 8.6 %copy-start.257 = (f32[1,256]{1,0:T(1,128)}, f32[1,256]{1,0:T(1,128)S(1)}, u32[]{:S(2)}) copy-start(f32[1,256]{1,0:T(1,128)S(1)} %get-tuple-element.195) | copy-start | bytes 3076
  23.1 42.2 %copy-start.261 = (f32[1,256]{1,0:T(1,128)}, f32[1,256]{1,0:T(1,128)S(1)}, u32[]{:S(2)}) copy-start(f32[1,256]{1,0:T(1,128)S(1)} %get-tuple-element.194) | copy-start | bytes 3076
  23.1 8.6 %copy-start.259 = (f32[1,256]{1,0:T(1,128)}, f32[1,256]{1,0:T(1,128)S(1)}, u32[]{:S(2)}) copy-start(f32[1,256]{1,0:T(1,128)S(1)} %get-tuple-element.200) | copy-start | bytes 3076
  23.1 42.2 %copy-start.263 = (f32[1,256]{1,0:T(1,128)}, f32[1,256]{1,0:T(1,128)S(1)}, u32[]{:S(2)}) copy-start(f32[1,256]{1,0:T(1,128)S(1)} %get-tuple-element.201) | copy-start | bytes 3076
  42.8 20.0 %copy-start.25 = (bf16[8,7,28,256]{3,2,1,0:T(8,128)(2,1)}, bf16[8,7,28,256]{3,2,1,0:T(8,128)(2,1)S(1)}, u32[]{:S(2)}) copy-start(bf16[8,7,28,256]{3,2,1,0:T(8,128)(2,1)S(1)} %get-tuple-element.193) | copy-start | bytes 2408452
  42.8 22.1 %copy-start.23 = (bf16[8,7,28,256]{3,2,1,0:T(8,128)(2,1)}, bf16[8,7,28,256]{3,2,1,0:T(8,128)(2,1)S(1)}, u32[]{:S(2)}) copy-start(bf16[8,7,28,256]{3,2,1,0:T(8,128)(2,1)S(1)} %get-tuple-element.192) | copy-start | bytes 2408452
  42.8 12.4 %collective-permute-start.2 = (bf16[8,1,28,256]{3,2,1,0:T(8,128)(2,1)S(1)}, bf16[8,1,28,256]{3,2,1,0:T(8,128)(2,1)S(1)}, u32[]{:S(2)}, u32[]{:S(2)}) collective-permute-start(bf16[8,1,28,256]{3,2,1,0:T(8,128)(2,1)S(1)} %get-tuple-element.153), channel_id=1, source_target_pairs={{0,1},{1,2},{2,3},{4,5},{5,6},{6,7},{8,9},{9,10},{10,11},{12,13},{... | collective-permute-start | bytes 344072 | tf_op jit(solution)/shard_map/ppermute | solution.py:22
  46.4 8.8 %collective-permute-start.3 = (bf16[8,1,28,256]{3,2,1,0:T(8,128)(2,1)S(1)}, bf16[8,1,28,256]{3,2,1,0:T(8,128)(2,1)S(1)}, u32[]{:S(2)}, u32[]{:S(2)}) collective-permute-start(bf16[8,1,28,256]{3,2,1,0:T(8,128)(2,1)S(1)} %get-tuple-element.154), channel_id=1, source_target_pairs={{1,0},{2,1},{3,2},{5,4},{6,5},{7,6},{9,8},{10,9},{11,10},{13,12},{... | collective-permute-start | bytes 344072 | tf_op jit(solution)/shard_map/ppermute | solution.py:23
  49.2 8.8 %collective-permute-start.6 = (bf16[8,1,28,256]{3,2,1,0:T(8,128)(2,1)S(1)}, bf16[8,1,28,256]{3,2,1,0:T(8,128)(2,1)S(1)}, u32[]{:S(2)}, u32[]{:S(2)}) collective-permute-start(bf16[8,1,28,256]{3,2,1,0:T(8,128)(2,1)S(1)} %get-tuple-element.157), channel_id=1, source_target_pairs={{0,1},{1,2},{2,3},{4,5},{5,6},{6,7},{8,9},{9,10},{10,11},{12,13},{... | collective-permute-start | bytes 344072 | tf_op jit(solution)/shard_map/ppermute | solution.py:22
  52.8 6.8 collective-permute-start.7
  55.2 9.2 %copy-start.149 = (bf16[8,1,28,256]{3,2,1,0:T(8,128)(2,1)}, bf16[8,1,28,256]{3,2,1,0:T(8,128)(2,1)S(1)}, u32[]{:S(2)}) copy-start(bf16[8,1,28,256]{3,2,1,0:T(8,128)(2,1)S(1)} %collective-permute-done.2) | copy-start | bytes 344068
  55.2 9.7 %copy-start.147 = (bf16[8,1,28,256]{3,2,1,0:T(8,128)(2,1)}, bf16[8,1,28,256]{3,2,1,0:T(8,128)(2,1)S(1)}, u32[]{:S(2)}) copy-start(bf16[8,1,28,256]{3,2,1,0:T(8,128)(2,1)S(1)} %collective-permute-done.3) | copy-start | bytes 344068
  55.9 9.4 %copy-start.15 = (bf16[8,9,30,256]{3,2,1,0:T(8,128)(2,1)}, bf16[8,9,30,256]{3,2,1,0:T(8,128)(2,1)S(1)}, u32[]{:S(2)}) copy-start(bf16[8,9,30,256]{3,2,1,0:T(8,128)(2,1)S(1)} %select_maximum_fusion.12) | copy-start | bytes 3317764
  65.7 12.0 %copy-start.275 = (bf16[256,512]{1,0:T(8,128)(2,1)S(1)}, bf16[256,512]{1,0:T(8,128)(2,1)}, u32[]{:S(2)}) copy-start(bf16[256,512]{1,0:T(8,128)(2,1)} %param.28) | copy-start | bytes 786436
  65.7 12.0 %copy-start.280 = (f32[512]{0:T(512)S(1)}, f32[512]{0:T(512)}, u32[]{:S(2)}) copy-start(f32[512]{0:T(512)} %param.29) | copy-start | bytes 6148
  79.7 107.2 %all-gather.5.cloned.1.call-start = ((), (), s32[]{:S(2)}) async-start(), calls=%async_computation.3 | async-start | bytes 9175040 | tf_op jit(solution)/shard_map/all_gather | solution.py:214
  81.7 298.7 %reduce-scatter.5.cloned.1.call-start = ((), (), s32[]{:S(2)}) async-start(), calls=%async_computation.5 | async-start | bytes 8028160 | tf_op jit(solution)/shard_map/reduce_scatter | solution.py:325
  87.3 124.8 %copy-start.29 = (f32[2,128,512]{2,1,0:T(8,128)}, f32[2,128,512]{2,1,0:T(8,128)S(1)}, u32[]{:S(2)}) copy-start(f32[2,128,512]{2,1,0:T(8,128)S(1)} %get-tuple-element.224) | copy-start | bytes 1572868
  87.4 124.8 %copy-start.183 = (f32[2,128]{1,0:T(2,128)}, f32[2,128]{1,0:T(2,128)S(1)}, u32[]{:S(2)}) copy-start(f32[2,128]{1,0:T(2,128)S(1)} %broadcast_multiply_fusion.2) | copy-start | bytes 3076
  87.6 124.5 %copy-start.198 = (f32[2,128]{1,0:T(2,128)}, f32[2,128]{1,0:T(2,128)S(1)}, u32[]{:S(2)}) copy-start(f32[2,128]{1,0:T(2,128)S(1)} %fusion.469) | copy-start | bytes 3076
  95.6 144.8 %copy-start.31 = (f32[2,128,512]{2,1,0:T(8,128)}, f32[2,128,512]{2,1,0:T(8,128)S(1)}, u32[]{:S(2)}) copy-start(f32[2,128,512]{2,1,0:T(8,128)S(1)} %get-tuple-element.213) | copy-start | bytes 1572868
  95.7 94.9 %copy-start.185 = (f32[2,128]{1,0:T(2,128)}, f32[2,128]{1,0:T(2,128)S(1)}, u32[]{:S(2)}) copy-start(f32[2,128]{1,0:T(2,128)S(1)} %broadcast_multiply_fusion.5) | copy-start | bytes 3076
  95.9 94.7 %copy-start.217 = (f32[2,128]{1,0:T(2,128)}, f32[2,128]{1,0:T(2,128)S(1)}, u32[]{:S(2)}) copy-start(f32[2,128]{1,0:T(2,128)S(1)} %multiply_reduce_fusion.23) | copy-start | bytes 3076
  95.9 94.7 %copy-start.200 = (f32[2,128]{1,0:T(2,128)}, f32[2,128]{1,0:T(2,128)S(1)}, u32[]{:S(2)}) copy-start(f32[2,128]{1,0:T(2,128)S(1)} %fusion.466) | copy-start | bytes 3076
  99.1 134.1 %copy-start.89 = (bf16[2,128,512]{1,2,0:T(8,128)(2,1)}, bf16[2,128,512]{1,2,0:T(8,128)(2,1)S(1)}, u32[]{:S(2)}) copy-start(bf16[2,128,512]{1,2,0:T(8,128)(2,1)S(1)} %copy.176) | copy-start | bytes 786436
  240.9 13.2 %copy-start.53 = (f32[2,128,512]{2,1,0:T(8,128)}, f32[2,128,512]{2,1,0:T(8,128)S(1)}, u32[]{:S(2)}) copy-start(f32[2,128,512]{2,1,0:T(8,128)S(1)} %get-tuple-element.217) | copy-start | bytes 1572868
  241.0 13.2 %copy-start.206 = (f32[2,128]{1,0:T(2,128)}, f32[2,128]{1,0:T(2,128)S(1)}, u32[]{:S(2)}) copy-start(f32[2,128]{1,0:T(2,128)S(1)} %broadcast_multiply_fusion.4) | copy-start | bytes 3076
  241.3 12.9 %copy-start.213 = (f32[2,128]{1,0:T(2,128)}, f32[2,128]{1,0:T(2,128)S(1)}, u32[]{:S(2)}) copy-start(f32[2,128]{1,0:T(2,128)S(1)} %fusion.467) | copy-start | bytes 3076
  256.6 7.7 slice-start.2
  288.8 120.9 %reduce-scatter.3.cloned.1.call-start = ((), (), s32[]{:S(2)}) async-start(), calls=%async_computation.4 | async-start | bytes 8028160 | tf_op jit(solution)/shard_map/reduce_scatter | solution.py:325
  324.0 459.1 %all-reduce.12.cloned.1.call-start = ((), (), s32[]{:S(2)}) async-start(), calls=%async_computation.6 | async-start | bytes 35651584 | tf_op jit(solution)/shard_map/psum | solution.py:363
  335.5 20.3 %copy-start.221 = (f32[2,128]{1,0:T(2,128)}, f32[2,128]{1,0:T(2,128)S(1)}, u32[]{:S(2)}) copy-start(f32[2,128]{1,0:T(2,128)S(1)} %negate_multiply_fusion.6) | copy-start | bytes 3076
  345.3 12.5 %copy-start.223 = (f32[2,128]{1,0:T(2,128)}, f32[2,128]{1,0:T(2,128)S(1)}, u32[]{:S(2)}) copy-start(f32[2,128]{1,0:T(2,128)S(1)} %negate_multiply_fusion.7) | copy-start | bytes 3076
  380.4 7.2 copy-start.22
  409.6 6.9 copy-start.16
  416.5 6.8 copy-start.26
  416.5 6.8 copy-start.28
  417.4 25.3 %collective-permute-start.13 = (bf16[8,1,28,256]{3,2,1,0:T(8,128)(2,1)S(1)}, bf16[8,1,28,256]{3,2,1,0:T(8,128)(2,1)S(1)}, u32[]{:S(2)}, u32[]{:S(2)}) collective-permute-start(bf16[8,1,28,256]{3,2,1,0:T(8,128)(2,1)S(1)} %copy-done.176), channel_id=1, source_target_pairs={{1,0},{2,1},{3,2},{5,4},{6,5},{7,6},{9,8},{10,9},{11,10},{13,12},{... | collective-permute-start | bytes 344072 | tf_op jit(solution)/shard_map/ppermute | solution.py:23
  420.1 22.6 %collective-permute-start.12 = (bf16[8,1,28,256]{3,2,1,0:T(8,128)(2,1)S(1)}, bf16[8,1,28,256]{3,2,1,0:T(8,128)(2,1)S(1)}, u32[]{:S(2)}, u32[]{:S(2)}) collective-permute-start(bf16[8,1,28,256]{3,2,1,0:T(8,128)(2,1)S(1)} %get-tuple-element.152), channel_id=1, source_target_pairs={{0,1},{1,2},{2,3},{4,5},{5,6},{6,7},{8,9},{9,10},{10,11},{12,13},{... | collective-permute-start | bytes 344072 | tf_op jit(solution)/shard_map/ppermute | solution.py:22
  427.5 20.6 %collective-permute-start.9 = (bf16[8,1,28,256]{3,2,1,0:T(8,128)(2,1)S(1)}, bf16[8,1,28,256]{3,2,1,0:T(8,128)(2,1)S(1)}, u32[]{:S(2)}, u32[]{:S(2)}) collective-permute-start(bf16[8,1,28,256]{3,2,1,0:T(8,128)(2,1)S(1)} %get-tuple-element.147), channel_id=1, source_target_pairs={{1,0},{2,1},{3,2},{5,4},{6,5},{7,6},{9,8},{10,9},{11,10},{13,12},{... | collective-permute-start | bytes 344072 | tf_op jit(solution)/shard_map/ppermute | solution.py:23
  439.1 9.1 %collective-permute-start.8 = (bf16[8,1,28,256]{3,2,1,0:T(8,128)(2,1)S(1)}, bf16[8,1,28,256]{3,2,1,0:T(8,128)(2,1)S(1)}, u32[]{:S(2)}, u32[]{:S(2)}) collective-permute-start(bf16[8,1,28,256]{3,2,1,0:T(8,128)(2,1)S(1)} %get-tuple-element.148), channel_id=1, source_target_pairs={{0,1},{1,2},{2,3},{4,5},{5,6},{6,7},{8,9},{9,10},{10,11},{12,13},{... | collective-permute-start | bytes 344072 | tf_op jit(solution)/shard_map/ppermute | solution.py:22
  454.5 8.7 %copy-start.5 = (bf16[8,9,30,256]{3,2,1,0:T(8,128)(2,1)S(1)}, bf16[8,9,30,256]{3,2,1,0:T(8,128)(2,1)}, u32[]{:S(2)}) copy-start(bf16[8,9,30,256]{3,2,1,0:T(8,128)(2,1)} %copy-done.4) | copy-start | bytes 3317764
  471.6 6.9 copy-start.14
  496.1 7.5 copy-start.38
  496.1 13.8 %copy-start.12 = (bf16[3,3,256,256]{3,2,1,0:T(8,128)(2,1)S(1)}, bf16[3,3,256,256]{3,2,1,0:T(8,128)(2,1)}, u32[]{:S(2)}) copy-start(bf16[3,3,256,256]{3,2,1,0:T(8,128)(2,1)} %copy-done.11) | copy-start | bytes 3538948
  498.0 58.0 %collective-permute-start.11 = (bf16[8,1,28,256]{3,2,1,0:T(8,128)(2,1)}, bf16[8,1,28,256]{3,2,1,0:T(8,128)(2,1)S(1)}, u32[]{:S(2)}, u32[]{:S(2)}) collective-permute-start(bf16[8,1,28,256]{3,2,1,0:T(8,128)(2,1)} %get-tuple-element.145), channel_id=1, source_target_pairs={{1,0},{2,1},{3,2},{5,4},{6,5},{7,6},{9,8},{10,9},{11,10},{13,12},{... | collective-permute-start | bytes 344072 | tf_op jit(solution)/shard_map/ppermute | solution.py:23
  499.9 56.1 %collective-permute-start.10 = (bf16[8,1,28,256]{3,2,1,0:T(8,128)(2,1)}, bf16[8,1,28,256]{3,2,1,0:T(8,128)(2,1)S(1)}, u32[]{:S(2)}, u32[]{:S(2)}) collective-permute-start(bf16[8,1,28,256]{3,2,1,0:T(8,128)(2,1)} %get-tuple-element.146), channel_id=1, source_target_pairs={{0,1},{1,2},{2,3},{4,5},{5,6},{6,7},{8,9},{9,10},{10,11},{12,13},{... | collective-permute-start | bytes 344072 | tf_op jit(solution)/shard_map/ppermute | solution.py:22
  504.3 52.4 %collective-permute-start.15 = (bf16[8,1,28,256]{3,2,1,0:T(8,128)(2,1)}, bf16[8,1,28,256]{3,2,1,0:T(8,128)(2,1)S(1)}, u32[]{:S(2)}, u32[]{:S(2)}) collective-permute-start(bf16[8,1,28,256]{3,2,1,0:T(8,128)(2,1)} %get-tuple-element.149), channel_id=1, source_target_pairs={{1,0},{2,1},{3,2},{5,4},{6,5},{7,6},{9,8},{10,9},{11,10},{13,12},{... | collective-permute-start | bytes 344072 | tf_op jit(solution)/shard_map/ppermute | solution.py:23
  506.2 50.5 %collective-permute-start.14 = (bf16[8,1,28,256]{3,2,1,0:T(8,128)(2,1)}, bf16[8,1,28,256]{3,2,1,0:T(8,128)(2,1)S(1)}, u32[]{:S(2)}, u32[]{:S(2)}) collective-permute-start(bf16[8,1,28,256]{3,2,1,0:T(8,128)(2,1)} %get-tuple-element.150), channel_id=1, source_target_pairs={{0,1},{1,2},{2,3},{4,5},{5,6},{6,7},{8,9},{9,10},{10,11},{12,13},{... | collective-permute-start | bytes 344072 | tf_op jit(solution)/shard_map/ppermute | solution.py:22
  (245 other events, 542.8 us)
Sparse Core Ops, SparseCore 0:
  79.8 52.5 all-gather.2
  134.5 52.3 all-gather.4
  288.9 58.8 reduce-scatter.4
  350.4 59.2 reduce-scatter.2
  488.1 294.9 all-reduce.11
where the time goes:
time: 820 us; the launch traced here: 808 us
  waiting for transfers between devices  315 us (38%)
  matrix products  221 us (27%)
  local copies, waits for them, and re-layouts  126 us (15%)
  starting transfers between devices  46.9 us (6%)
  blocking collectives  41.6 us (5%)
  other arithmetic  39.2 us (5%)
  between operations  18 us (2%)
    psum x1, waiting for transfers between devices, body(): lax.psum((running[0], running[1], running[2], running[3], running[4], run...  206 us
    all_gather x2, waiting for transfers between devices, body(): every = lax.all_gather(tokens, 'row', axis=1, tiled=True)  87.7 us
    unnamed x585, local copies, waits for them, and re-layouts  56.7 us
    dot_general x36, matrix products, conv_back(): jnp.einsum('grwd,cd->grwc', window, kernel[step_a, step_b], preferred_ele...  45.8 us
    psum x1, blocking collectives, body(): lax.psum((running[0], running[1], running[2], running[3], running[4], run...  41.6 us
    dot_general x36, matrix products, conv_rows(): jnp.einsum('grwc,cd->grwd', window, kernel[step_a, step_b], preferred_ele...  37.2 us
    ppermute x8, starting transfers between devices, padded_2(): before = lax.ppermute(last, axis, up)  29.8 us
    reduce_scatter x2, waiting for transfers between devices, body(): lax.psum_scatter(placed.astype(jnp.bfloat16), 'row', scatter_dimension=1,...  19.2 us
  transfers between devices with their start and end apart: 21, of which 5 were waited for; matrix products, arithmetic and copies ran while one was open for 20% of the time, Pallas kernels for 0%

commit v1 on v0

v1 whole, which is shorter than its diff:
```python
import math

import jax
import jax.numpy as jnp
from jax import lax
from jax.sharding import PartitionSpec as P

HEADS = 8


EPS = 1e-05
MASKED = -1e30


def layer_norm(inputs, scaling, offset):
    center = inputs - jnp.mean(inputs, -1, keepdims=True)
    spread = jnp.mean(center * center, -1, keepdims=True)
    return center * lax.rsqrt(spread + EPS) * scaling + offset


def smooth(inputs):
    return jax.nn.gelu(inputs, approximate=False)


def smooth_grad(inputs, upstream):
    return jax.vjp(smooth, inputs)[1](upstream)[0]


def norm_grad(inputs, scaling, offset, upstream):
    pullback = jax.vjp(layer_norm, inputs, scaling, offset)[1]
    return pullback(upstream)


def conv_fwd(inputs, kernel):
    return lax.conv_general_dilated(
        inputs, kernel, (1, 1), ((1, 1), (1, 1)),
        dimension_numbers=("NHWC", "HWIO", "NHWC"), preferred_element_type=jnp.float32,
    )


def conv_back(upstream, kernel):
    return lax.conv_general_dilated(
        upstream, kernel[::-1, ::-1], (1, 1), ((1, 1), (1, 1)),
        dimension_numbers=("NHWC", "HWOI", "NHWC"), preferred_element_type=jnp.float32,
    )


def kernel_grad(inputs, upstream):
    return lax.conv_general_dilated(
        inputs, upstream, (1, 1), ((1, 1), (1, 1)),
        dimension_numbers=("CHWN", "IHWO", "HWNC"), preferred_element_type=jnp.float32,
    )

def head_view(matrix):
    return matrix.reshape(matrix.shape[0], matrix.shape[1], HEADS, matrix.shape[2] // HEADS)


def scores_of(queries, keys_in, allowed, scale):
    scores = (
        jnp.einsum(
            "oqhe,okhe->ohqk",
            head_view(queries),
            head_view(keys_in),
            preferred_element_type=jnp.float32,
        )
        * scale
    )
    if allowed is None:
        return scores
    return jnp.where(allowed, scores, MASKED)


def attend(queries, keys_in, values_in, allowed, scale):
    scores = scores_of(queries, keys_in, allowed, scale)
    highest = jnp.max(scores, -1, keepdims=True)
    raised = jnp.exp(scores - highest)
    totals = jnp.sum(raised, -1, keepdims=True)
    shares = raised / totals
    logsum = highest + jnp.log(totals)
    mixed = jnp.einsum(
        "ohqk,okhe->oqhe",
        shares.astype(jnp.bfloat16),
        head_view(values_in),
        preferred_element_type=jnp.float32,
    )
    return (mixed.reshape(queries.shape).astype(jnp.bfloat16), logsum)


def attend_back(queries, keys_in, values_in, allowed, scale, logsum, upstream):
    scores = scores_of(queries, keys_in, allowed, scale)
    shares = jnp.exp(scores - logsum)
    up_heads = head_view(upstream)
    grad_shares = jnp.einsum(
        "oqhe,okhe->ohqk", up_heads, head_view(values_in), preferred_element_type=jnp.float32
    )
    grad_scores = (
        shares * (grad_shares - jnp.sum(grad_shares * shares, -1, keepdims=True))
    ).astype(jnp.bfloat16)
    grad_query = (
        jnp.einsum(
            "ohqk,okhe->oqhe", grad_scores, head_view(keys_in), preferred_element_type=jnp.float32
        )
        * scale
    )
    grad_key = (
        jnp.einsum(
            "ohqk,oqhe->okhe", grad_scores, head_view(queries), preferred_element_type=jnp.float32
        )
        * scale
    )
    grad_value = jnp.einsum(
        "ohqk,oqhe->okhe", shares.astype(jnp.bfloat16), up_heads, preferred_element_type=jnp.float32
    )
    return (
        grad_query.reshape(queries.shape),
        grad_key.reshape(keys_in.shape),
        grad_value.reshape(values_in.shape),
    )


def body(
    image,
    tags,
    tag_lengths,
    cotangent,
    conv_weight,
    bn_mean,
    bn_var,
    bn_scale,
    bn_shift,
    proj_weight,
    proj_bias,
    attn_in,
    attn_out,
    ln_gain,
    ln_bias,
    ffn_in,
    ffn_in_bias,
    ffn_out,
    ffn_out_bias,
):
    batches = image.shape[0]
    owned = tags.shape[1]
    slots = tags.shape[2]
    scale = 1.0 / math.sqrt(tags.shape[3] // HEADS)
    factor = lax.rsqrt(bn_var + EPS)
    position = jnp.arange(slots)
    causal = (position[None, :] <= position[:, None])[None, None]
    tables = batches * owned
    moved = lax.all_to_all(image, "row", 1, 2, tiled=True)
    inputs = moved.reshape((tables,) + moved.shape[2:])
    pre_one = conv_fwd(inputs, conv_weight[0])
    norm_one = (pre_one - bn_mean[0]) * factor[0]
    act_one = norm_one * bn_scale[0] + bn_shift[0]
    hidden = smooth(act_one).astype(jnp.bfloat16)
    pre_two = conv_fwd(hidden, conv_weight[1])
    norm_two = (pre_two - bn_mean[1]) * factor[1]
    act_two = norm_two * bn_scale[1] + bn_shift[1] + inputs.astype(jnp.float32)
    block_out = smooth(act_two).astype(jnp.bfloat16)
    tokens = (
        jnp.einsum("grwc,cd->grwd", block_out, proj_weight, preferred_element_type=jnp.float32)
        + proj_bias
    ).astype(jnp.bfloat16)
    memory = tokens.reshape(tables, -1, tokens.shape[-1])
    start = tags.reshape((tables,) + tags.shape[2:])
    lengths = tag_lengths.reshape(-1)
    allowed = causal & (position[None, :] < lengths[:, None])[:, None, None, :]
    projected = jnp.einsum(
        "old,jde->jole", start, attn_in[:3], preferred_element_type=jnp.float32
    ).astype(jnp.bfloat16)
    self_mix, self_log = attend(projected[0], projected[1], projected[2], allowed, scale)
    first_in = start.astype(jnp.float32) + jnp.einsum(
        "old,de->ole", self_mix, attn_out[0], preferred_element_type=jnp.float32
    )
    first = layer_norm(first_in, ln_gain[0], ln_bias[0])
    first_b = first.astype(jnp.bfloat16)
    cross_q = jnp.einsum(
        "old,de->ole", first_b, attn_in[3], preferred_element_type=jnp.float32
    ).astype(jnp.bfloat16)
    cross_kv = jnp.einsum(
        "oid,jde->joie", memory, attn_in[4:6], preferred_element_type=jnp.float32
    ).astype(jnp.bfloat16)
    cross_mix, cross_log = attend(cross_q, cross_kv[0], cross_kv[1], None, scale)
    second_in = first + jnp.einsum(
        "old,de->ole", cross_mix, attn_out[1], preferred_element_type=jnp.float32
    )
    second = layer_norm(second_in, ln_gain[1], ln_bias[1])
    second_b = second.astype(jnp.bfloat16)
    inner = (
        jnp.einsum("old,df->olf", second_b, ffn_in, preferred_element_type=jnp.float32)
        + ffn_in_bias
    )
    inner_act = smooth(inner).astype(jnp.bfloat16)
    third_in = (
        second
        + jnp.einsum("olf,fd->old", inner_act, ffn_out, preferred_element_type=jnp.float32)
        + ffn_out_bias
    )
    decoded = layer_norm(third_in, ln_gain[2], ln_bias[2]).astype(jnp.bfloat16)
    grad_third, gain_three, shift_three = norm_grad(
        third_in, ln_gain[2], ln_bias[2], cotangent.reshape(start.shape).astype(jnp.float32)
    )
    grad_outer = grad_third.astype(jnp.bfloat16)
    ffn_out_g = jnp.einsum(
        "olf,old->fd", inner_act, grad_outer, preferred_element_type=jnp.float32
    )
    ffn_out_bias_g = jnp.sum(grad_outer.astype(jnp.float32), axis=(0, 1))
    grad_act = jnp.einsum(
        "old,fd->olf", grad_outer, ffn_out, preferred_element_type=jnp.float32
    )
    grad_inner = smooth_grad(inner, grad_act).astype(jnp.bfloat16)
    ffn_in_g = jnp.einsum(
        "old,olf->df", second_b, grad_inner, preferred_element_type=jnp.float32
    )
    ffn_in_bias_g = jnp.sum(grad_inner.astype(jnp.float32), axis=(0, 1))
    grad_second = grad_third + jnp.einsum(
        "olf,df->old", grad_inner, ffn_in, preferred_element_type=jnp.float32
    )
    grad_second_in, gain_two, shift_two = norm_grad(
        second_in, ln_gain[1], ln_bias[1], grad_second
    )
    grad_cross_out = grad_second_in.astype(jnp.bfloat16)
    out_two_g = jnp.einsum(
        "old,ole->de", cross_mix, grad_cross_out, preferred_element_type=jnp.float32
    )
    grad_cross_mix = jnp.einsum(
        "ole,de->old", grad_cross_out, attn_out[1], preferred_element_type=jnp.float32
    ).astype(jnp.bfloat16)
    cross_grads = attend_back(
        cross_q, cross_kv[0], cross_kv[1], None, scale, cross_log, grad_cross_mix
    )
    grad_cross_q = cross_grads[0].astype(jnp.bfloat16)
    grad_cross_kv = jnp.stack([cross_grads[1], cross_grads[2]]).astype(jnp.bfloat16)
    in_three_g = jnp.einsum(
        "old,ole->de", first_b, grad_cross_q, preferred_element_type=jnp.float32
    )
    in_pair_g = jnp.einsum(
        "oid,joie->jde", memory, grad_cross_kv, preferred_element_type=jnp.float32
    )
    grad_memory = jnp.einsum(
        "joie,jde->oid", grad_cross_kv, attn_in[4:6], preferred_element_type=jnp.float32
    )
    grad_first = grad_second_in + jnp.einsum(
        "ole,de->old", grad_cross_q, attn_in[3], preferred_element_type=jnp.float32
    )
    grad_first_in, gain_one, shift_one = norm_grad(first_in, ln_gain[0], ln_bias[0], grad_first)
    grad_self_out = grad_first_in.astype(jnp.bfloat16)
    out_one_g = jnp.einsum(
        "old,ole->de", self_mix, grad_self_out, preferred_element_type=jnp.float32
    )
    grad_self_mix = jnp.einsum(
        "ole,de->old", grad_self_out, attn_out[0], preferred_element_type=jnp.float32
    ).astype(jnp.bfloat16)
    self_grads = attend_back(
        projected[0], projected[1], projected[2], allowed, scale, self_log, grad_self_mix
    )
    grad_projected = jnp.stack([self_grads[0], self_grads[1], self_grads[2]]).astype(
        jnp.bfloat16
    )
    in_self_g = jnp.einsum(
        "old,jole->jde", start, grad_projected, preferred_element_type=jnp.float32
    )
    tags_grad = (
        grad_first_in
        + jnp.einsum(
            "jole,jde->old", grad_projected, attn_in[:3], preferred_element_type=jnp.float32
        )
    )
    grad_tokens = grad_memory.reshape(tokens.shape).astype(jnp.bfloat16)
    proj_g = jnp.einsum(
        "grwc,grwd->cd", block_out, grad_tokens, preferred_element_type=jnp.float32
    )
    proj_bias_g = jnp.sum(grad_tokens.astype(jnp.float32), axis=(0, 1, 2))
    grad_block = jnp.einsum(
        "grwd,cd->grwc", grad_tokens, proj_weight, preferred_element_type=jnp.float32
    )
    grad_act_two = smooth_grad(act_two, grad_block)
    scale_two_g = jnp.sum(grad_act_two * norm_two, axis=(0, 1, 2))
    shift_two_g = jnp.sum(grad_act_two, axis=(0, 1, 2))
    grad_pre_two = (grad_act_two * bn_scale[1] * factor[1]).astype(jnp.bfloat16)
    conv_two_g = kernel_grad(hidden, grad_pre_two)
    grad_hidden = conv_back(grad_pre_two, conv_weight[1])
    grad_act_one = smooth_grad(act_one, grad_hidden)
    scale_one_g = jnp.sum(grad_act_one * norm_one, axis=(0, 1, 2))
    shift_one_g = jnp.sum(grad_act_one, axis=(0, 1, 2))
    grad_pre_one = (grad_act_one * bn_scale[0] * factor[0]).astype(jnp.bfloat16)
    conv_one_g = kernel_grad(inputs, grad_pre_one)
    image_grad = conv_back(grad_pre_one, conv_weight[0]) + grad_act_two
    local = (
        jnp.stack([conv_one_g, conv_two_g]),
        jnp.stack([scale_one_g, scale_two_g]),
        jnp.stack([shift_one_g, shift_two_g]),
        proj_g,
        proj_bias_g,
        jnp.concatenate([in_self_g, in_three_g[None], in_pair_g]),
        jnp.stack([out_one_g, out_two_g]),
        jnp.stack([gain_one, gain_two, gain_three]),
        jnp.stack([shift_one, shift_two, shift_three]),
        ffn_in_g,
        ffn_in_bias_g,
        ffn_out_g,
        ffn_out_bias_g,
    )
    wide = [0, 3, 5, 6, 9, 11]
    sent = [g.astype(jnp.bfloat16) if i in wide else g for i, g in enumerate(local)]
    big = lax.psum(tuple(sent[i] for i in wide), ("dp", "row"))
    rest = [i for i in range(len(sent)) if i not in wide]
    small = lax.psum(jnp.concatenate([sent[i].reshape(-1) for i in rest]), ("dp", "row"))
    summed = list(local)
    for i, g in zip(wide, big):
        summed[i] = g.astype(jnp.float32)
    at = 0
    for i in rest:
        summed[i] = small[at : at + local[i].size].reshape(local[i].shape)
        at += local[i].size
    back = image_grad.astype(jnp.bfloat16).reshape((batches, owned) + image_grad.shape[1:])
    back = lax.all_to_all(back, "row", 2, 1, tiled=True)
    return (
        decoded.reshape(tags.shape),
        back.astype(jnp.float32),
        tags_grad.reshape(tags.shape),
        *summed,
    )


def solution(mesh):
    placed = (
        P(None, "dp", "row", None, None),
        P(None, ("dp", "row"), None, None),
        P(None, ("dp", "row")),
        P(None, ("dp", "row"), None, None),
        P(),
        P(),
        P(),
        P(),
        P(),
        P(),
        P(),
        P(),
        P(),
        P(),
        P(),
        P(),
        P(),
        P(),
        P(),
    )
    return jax.shard_map(
        body,
        mesh=mesh,
        in_specs=placed,
        out_specs=(
            P(None, ("dp", "row"), None, None),
            P(None, "dp", "row", None, None),
            P(None, ("dp", "row"), None, None),
            P(),
            P(),
            P(),
            P(),
            P(),
            P(),
            P(),
            P(),
            P(),
            P(),
            P(),
            P(),
            P(),
        ),
        check_vma=False,
    )
```

time: 820 us -> 530 us (0.65)
  waiting for transfers between devices: 315 us -> 85.6 us
  matrix products: 221 us -> 142 us
  starting transfers between devices: 46.9 us -> 9.2 us
  local copies, waits for them, and re-layouts: 126 us -> 150 us
  other arithmetic: 39.2 us -> 61.7 us
  blocking collectives: 41.6 us -> 57.5 us
    psum x1, waiting for transfers between devices: 206 us -> 74.9 us  [body(): big = lax.psum(tuple((sent[i] for i in wide)), ('dp', 'row'))]
    dot_general x108 -> x0, matrix products: 100 us -> none  [the longest x36 45.8 us: conv_back(): jnp.einsum('grwd,cd->grwc', window, kernel[step_a, step_b], preferred_ele...]
    all_gather x2 -> x0, waiting for transfers between devices: 87.7 us -> none  [body(): every = lax.all_gather(tokens, 'row', axis=1, tiled=True)]
    conv_general_dilated x0 -> x6, matrix products: none -> 49.7 us  [the longest x2 21.8 us: conv_fwd(): lax.conv_general_dilated(inputs, kernel, (1, 1), ((1, 1), (1, 1)), dimens...]
    ppermute x16 -> x0, starting transfers between devices: 46.3 us -> none  [the longest x8 29.8 us: padded_2(): before = lax.ppermute(last, axis, up)]
    unnamed x585 -> x251, local copies, waits for them, and re-layouts: 56.7 us -> 22 us
    reshape x0 -> x12, local copies, waits for them, and re-layouts: none -> 25.3 us  [the longest x9 22.5 us: body(): inputs = moved.reshape((tables,) + moved.shape[2:])]
    convert_element_type x0 -> x10, other arithmetic: none -> 22.5 us  [the longest x1 10.8 us: body(): block_out = smooth(act_two).astype(jnp.bfloat16)]
  transfers between devices with their start and end apart: 21 -> 3, of which waited for: 5 -> 2; matrix products, arithmetic and copies ran while one was open for 20% -> 12% of each run, Pallas kernels for 0% -> 0%
where the time goes in v1:
time: 530 us; the launch traced here: 522 us
  local copies, waits for them, and re-layouts  150 us (28%)
  matrix products  142 us (27%)
  waiting for transfers between devices  85.6 us (16%)
  other arithmetic  61.7 us (12%)
  blocking collectives  57.5 us (11%)
  between operations  15.9 us (3%)
  starting transfers between devices  9.2 us (2%)
    psum x1, waiting for transfers between devices, body(): big = lax.psum(tuple((sent[i] for i in wide)), ('dp', 'row'))  74.9 us
    psum x1, blocking collectives, body(): lax.psum(jnp.concatenate([sent[i].reshape(-1) for i in rest]), ('dp', 'ro...  57.5 us
    reshape x9, local copies, waits for them, and re-layouts, body(): inputs = moved.reshape((tables,) + moved.shape[2:])  22.5 us
    unnamed x251, local copies, waits for them, and re-layouts  22 us
    conv_general_dilated x2, matrix products, conv_fwd(): lax.conv_general_dilated(inputs, kernel, (1, 1), ((1, 1), (1, 1)), dimens...  21.8 us
    conv_general_dilated x2, matrix products, conv_back(): lax.conv_general_dilated(upstream, kernel[::-1, ::-1], (1, 1), ((1, 1), (...  18 us
    dot_general x2, matrix products, attend_back(): jnp.einsum('oqhe,okhe->ohqk', up_heads, head_view(values_in), preferred_e...  15.9 us
    conv_general_dilated x4, local copies, waits for them, and re-layouts, conv_back(): lax.conv_general_dilated(upstream, kernel[::-1, ::-1], (1, 1), ((1, 1), (...  13.9 us
  transfers between devices with their start and end apart: 3, of which 2 were waited for; matrix products, arithmetic and copies ran while one was open for 12% of the time, Pallas kernels for 0%

profile of v1, /device:TPU:1, one launch (start us, length us, event | category | flops | bytes accessed | tf_op | source)
XLA Modules:
  0.0 522.4 jit_solution(11652008996886948893)
XLA Ops:
  7.2 3.2 copy.133
  10.4 4.4 all-to-all-start
  14.9 2.4 fusion.108
  21.4 2.4 convolution_convert_fusion.3
  26.5 10.7 %all-to-all-done = bf16[2,8,7,28,256]{4,3,2,0,1:T(8,128)(2,1)} async-done(((bf16[2,8,7,28,256]{4,3,2,0,1:T(8,128)(2,1)}), bf16[2,8,7,28,256]{4,3,2,0,1:T(8,128)(2,1)}, u32[]{:S(2)}, u32[]{:S(2)}) %all-to-all-start) | async-done | bytes 1605664 | tf_op jit(solution)/shard_map/all_to_all | solution.py:150
  40.1 3.1 fusion.228
  43.2 4.3 reshape.316
  47.4 2.0 copy.136
  49.8 14.8 %fusion.87 = (bf16[28,32,4,256]{3,1,2,0:T(8,128)(2,1)S(1)}, f32[28,32,4,256]{3,1,2,0:T(8,128)}, f32[28,32,4,256]{3,1,2,0:T(8,128)}) fusion(pred[32,4]{0,1:T(4,128)(4,1)S(1)} %copy-done.107, f32[256]{0:T(256)S(1)} %bitcast.468, f32[256]{0:T(256)S(1)} %bitcast.455, f32[256]{0:T(256)S(1)} %bitcast.451, f32[256]{0:T(256)S(1)} %bitcast.466, ...), kind=kOutput, calls=%fused_computation.162 | convolution fusion | flops 4200595456 | bytes 13111808 | tf_op jit(solution)/shard_map/conv_general_dilated | solution.py:35
  65.0 7.0 %multiply_add_fusion = (f32[28,32,4,256]{3,1,2,0:T(8,128)S(1)}, f32[28,32,4,256]{3,1,2,0:T(8,128)}) fusion(f32[256]{0:T(256)S(1)} %bitcast.473, f32[256]{0:T(256)S(1)} %bitcast.449, f32[256]{0:T(256)S(1)} %bitcast.447, f32[256]{0:T(256)S(1)} %bitcast.472, bf16[2,3,3,256,256]{4,3,2,1,0:T(8,128)(2,1)S(1)} %copy-done.109, ...), kind=kOutput, calls=%fused_computation.56 | convolution fusion | flops 4139122688 | bytes 11276288 | tf_op jit(solution)/shard_map/conv_general_dilated | solution.py:35
  72.0 4.9 copy.137
  76.9 5.1 reshape.357
  82.0 10.8 %multiply_convert_fusion.5 = (bf16[4,28,28,256]{3,2,1,0:T(8,128)(2,1)S(1)}, f32[4,28,28,256]{3,2,1,0:T(8,128)}) fusion(bf16[4,28,28,256]{3,2,1,0:T(8,128)(2,1)} %bitcast.385, f32[28,4,32,256]{3,2,1,0:T(8,128)} %reshape.357), kind=kLoop, calls=%fused_computation.74 | loop fusion | flops 53788672 | bytes 10092544 | tf_op jit(solution)/shard_map/convert_element_type | solution.py:159
  95.1 3.0 copy.139
  98.1 5.8 %convert_bitcast_fusion = bf16[2,4,784,512]{3,2,0,1:T(8,128)(2,1)S(1)} fusion(bf16[4,784,512,1]{2,0,1,3:T(4,128)(2,1)S(1)} %bitcast.406, bf16[6,512,512]{2,1,0:T(8,128)(2,1)} %param.30), kind=kOutput, calls=%fused_computation.18 | convolution fusion | flops 3291545600 | bytes 10682368 | tf_op jit(solution)/shard_map/oid,jde->joie/dot_general | solution.py:180
  103.9 3.1 fusion.225
  107.0 5.7 %copy.143 = bf16[1,4,784,512]{2,3,1,0:T(8,128)(2,1)} copy(bf16[1,4,784,512]{3,2,0,1:T(8,128)(2,1)} %get-tuple-element.98) | data formatting | bytes 6422528 | tf_op jit(solution)/shard_map/slice | solution.py:183
  112.7 6.2 %copy.141 = bf16[1,4,784,512]{2,3,1,0:T(8,128)(2,1)} copy(bf16[1,4,784,512]{3,2,0,1:T(8,128)(2,1)} %get-tuple-element.99) | data formatting | bytes 6422528 | tf_op jit(solution)/shard_map/slice | solution.py:183
  119.0 4.3 multiply_reduce_fusion.1
  123.3 2.4 fusion
  125.6 2.3 copy-done.2
  128.0 5.2 fusion.142
  135.5 5.0 multiply_convert_fusion.7
  144.8 2.0 convert_reduce_fusion.1
  146.8 1.9 bitcast_convert_fusion.4
  152.9 14.0 %multiply_reduce_fusion = (f32[4,8,128]{2,1,0:T(8,128)S(1)}, f32[4,8,128,784]{2,3,1,0:T(8,128)}) fusion(f32[4,8,128,784]{2,3,1,0:T(8,128)} %copy-done.2, f32[4,8,128]{2,1,0:T(8,128)S(1)} %log_add_fusion.1, bf16[4,128,8,64]{1,3,2,0:T(8,128)(2,1)S(1)} %bitcast.396, bf16[4,784,8,64]{1,3,2,0:T(8,128)(2,1)} %bitcast.383), kind=kOutput, calls=%fused_computation.1 | convolution fusion | flops 423882752 | bytes 29458432 | tf_op jit(solution)/shard_map/oqhe,okhe->ohqk/dot_general | solution.py:93
  167.0 7.2 %multiply_convert_fusion = bf16[4,8,128,784]{2,3,1,0:T(8,128)(2,1)S(1)} fusion(f32[4,8,128,784]{2,3,1,0:T(8,128)} %get-tuple-element.153, f32[4,8,128,784]{2,3,1,0:T(8,128)S(1)} %bitcast.378, f32[4,8,128]{2,1,0:T(8,128)S(1)} %get-tuple-element.152, f32[4,8,128]{2,1,0:T(8,128)S(1)} %log_add_fusion.1), kind=kLoop, calls=%fused_computation | loop fusion | flops 16056320 | bytes 32145408 | tf_op jit(solution)/shard_map/convert_element_type | solution.py:98
  175.8 4.1 multiply_convert_fusion.1
  179.8 4.4 fusion.72
  184.3 3.1 reshape.347
  187.4 4.4 fusion.226
  191.8 2.6 fusion.227
  195.9 5.9 %copy.146 = bf16[1,4,784,512]{3,2,0,1:T(8,128)(2,1)} copy(bf16[1,4,784,512]{2,3,1,0:T(8,128)(2,1)} %bitcast.381) | data formatting | bytes 6422528 | tf_op jit(solution)/shard_map/stack;reshape | solution.py:233
  201.8 6.3 %copy.147 = bf16[1,4,784,512]{3,2,0,1:T(8,128)(2,1)} copy(bf16[1,4,784,512]{2,3,1,0:T(8,128)(2,1)} %bitcast.387) | data formatting | bytes 6422528 | tf_op jit(solution)/shard_map/stack;reshape | solution.py:233
  208.1 7.4 %convert_reduce_fusion = (f32[512]{0:T(512)}, bf16[4,784,512]{2,1,0:T(8,128)(2,1)S(1)}) fusion(bf16[6,512,512]{2,1,0:T(8,128)(2,1)} %param.30, bf16[1,4,784,512]{3,2,0,1:T(8,128)(2,1)} %copy.147, bf16[1,4,784,512]{3,2,0,1:T(8,128)(2,1)} %copy.146), kind=kOutput, calls=%fused_computation.15 | convolution fusion | flops 3296361984 | bytes 10684416 | tf_op jit(solution)/shard_map/joie,jde->oid/dot_general | solution.py:240
  215.5 2.5 copy.148
  218.1 2.6 multiply_add_fusion.2
  221.3 2.4 pad.7
  227.4 2.0 multiply_reduce_fusion.4
  232.7 2.1 copy.156
  243.6 4.7 fusion.129
  251.9 3.1 reshape.336
  255.8 3.3 fusion.23
  259.1 4.1 fusion.84
  267.8 3.2 copy.167
  276.3 11.6 %select_reduce_fusion.1 = (f32[256]{0:T(256)S(1)}, f32[256]{0:T(256)S(1)}, f32[28,32,4,256]{3,1,2,0:T(8,128)S(1)}) fusion(pred[32,4]{0,1:T(4,128)(4,1)S(1)} %copy-done.108, f32[256]{0:T(256)S(1)} %bitcast.452, f32[256]{0:T(256)S(1)} %bitcast.467, f32[28,32,4,256]{3,1,2,0:T(8,128)} %get-tuple-element.137, f32[28,32,4,256]{3,1,2,0:T(8,128)} %get-tuple-element.97, ...), kind=kOutput, calls=%fused_computation.54 | convolution fusion | flops 4149214720 | bytes 15865984 | tf_op jit(solution)/shard_map/conv_general_dilated | solution.py:42
  293.0 5.1 fusion.112
  298.1 4.8 fusion.117
  306.7 2.1 pad_maximum_fusion.4
  309.6 6.5 %fusion.48 = f32[28,32,4,256]{3,1,2,0:T(8,128)S(1)} fusion(bf16[28,4,7,1,256]{4,2,1,3,0:T(8,128)(2,1)S(1)} %get-tuple-element.110, bf16[28,4,7,1,256]{4,2,1,3,0:T(8,128)(2,1)S(1)} %get-tuple-element.109, bf16[28,4,8,4,256]{4,2,1,3,0:T(8,128)(2,1)S(1)} %fusion.192, bf16[2,3,3,256,256]{4,3,2,1,0:T(8,128)(2,1)} %param.23), kind=kOutput, calls=%fused_computation.103 | convolution fusion | flops 4140957696 | bytes 7487488 | tf_op jit(solution)/shard_map/conv_general_dilated | solution.py:42
  316.1 4.9 copy.151
  321.0 5.2 reshape.359
  326.2 7.0 %copy.173 = f32[28,32,4,256]{3,2,1,0:T(4,128)} copy(f32[28,32,4,256]{3,1,2,0:T(8,128)} %get-tuple-element.139) | data formatting | bytes 7340032 | tf_op jit(solution)/shard_map/mul | solution.py:157
  333.1 5.2 reshape.361
  338.4 5.0 fusion.218
  343.6 2.8 copy.153
  346.4 4.8 all-to-all-start.1
  351.3 57.5 %psum.50 = f32[6144]{0:T(1024)S(1)} all-reduce(f32[6144]{0:T(1024)S(1)} %constant_dynamic-update-slice_fusion), channel_id=1, replica_groups=mesh['dp'=8,'row'=4] {'dp','row'}, use_global_device_ids=true, to_apply=%region_32.33 | all-reduce | flops 6144 | bytes 49152 | tf_op jit(solution)/shard_map/psum | solution.py:308
  412.4 3.8 fusion.133
  417.9 3.3 copy.154
  421.2 5.3 %reshape.363 = f32[2,8,7,28,256]{4,1,3,2,0:T(8,128)} reshape(f32[2,4,2,7,28,256]{5,2,1,4,3,0:T(2,128)} %copy.154) | data formatting | bytes 6422528 | tf_op jit(solution)/shard_map/convert_element_type | solution.py:320
  426.5 74.9 %all-reduce.3.cloned.1.call-done = (bf16[6,512,512]{1,2,0:T(8,128)(2,1)}, bf16[2,3,3,256,256]{4,3,2,1,0:T(8,128)(2,1)}, bf16[256,512]{1,0:T(8,128)(2,1)}, bf16[2...) async-done(((bf16[6,512,512]{1,2,0:T(8,128)(2,1)}, bf16[2,3,3,256,256]{4,3,2,1,0:T(8,128)(2,1)}, bf16[256,512]{1,0:T(8,128)(2,1)}, ...) | async-done | bytes 8912912 | tf_op jit(solution)/shard_map/psum | solution.py:306
  501.4 5.5 %copy.183 = f32[6,512,512]{2,1,0:T(8,128)} copy(bf16[6,512,512]{1,2,0:T(8,128)(2,1)} %get-tuple-element.78) | data formatting | bytes 9437184
  506.9 2.7 convert_element_type.236
  (354 shorter events, 77.3 us)
Async XLA Ops:
  7.2 126.9 %copy-start = (bf16[512,1024]{1,0:T(8,128)(2,1)S(1)}, bf16[512,1024]{1,0:T(8,128)(2,1)}, u32[]{:S(2)}) copy-start(bf16[512,1024]{1,0:T(8,128)(2,1)} %param.34) | copy-start | bytes 3145732
  7.2 7.7 %copy-start.77 = (bf16[2,2,128,512]{3,2,1,0:T(8,128)(2,1)S(1)}, bf16[2,2,128,512]{3,2,1,0:T(8,128)(2,1)}, u32[]{:S(2)}) copy-start(bf16[2,2,128,512]{3,2,1,0:T(8,128)(2,1)} %param.20) | copy-start | bytes 1572868
  10.4 26.8 %all-to-all-start = ((bf16[2,8,7,28,256]{4,3,2,0,1:T(8,128)(2,1)}), bf16[2,8,7,28,256]{4,3,2,0,1:T(8,128)(2,1)}, u32[]{:S(2)}, u32[]{:S(2)}) async-start(bf16[2,8,7,28,256]{4,3,2,0,1:T(8,128)(2,1)} %copy.133), calls=%async_computation | async-start | bytes 3670016 | tf_op jit(solution)/shard_map/all_to_all | solution.py:150
  14.8 486.5 %all-reduce.3.cloned.1.call-start = ((), (), s32[]{:S(2)}) async-start(), calls=%async_computation.2 | async-start | bytes 17825792 | tf_op jit(solution)/shard_map/psum | solution.py:306
  19.7 5.4 %copy-start.98 = (f32[2,256]{1,0:T(2,128)S(1)}, f32[2,256]{1,0:T(2,128)}, u32[]{:S(2)}) copy-start(f32[2,256]{1,0:T(2,128)} %param.25) | copy-start | bytes 6148
  19.7 5.4 %copy-start.27 = (bf16[2,2,128,512]{3,2,1,0:T(8,128)(2,1)S(1)}, bf16[2,2,128,512]{3,2,1,0:T(8,128)(2,1)}, u32[]{:S(2)}) copy-start(bf16[2,2,128,512]{3,2,1,0:T(8,128)(2,1)} %param.22) | copy-start | bytes 1572868
  20.5 5.3 %copy-start.99 = (f32[2,256]{1,0:T(2,128)S(1)}, f32[2,256]{1,0:T(2,128)}, u32[]{:S(2)}) copy-start(f32[2,256]{1,0:T(2,128)} %param.26) | copy-start | bytes 6148
  20.5 5.3 %copy-start.100 = (f32[2,256]{1,0:T(2,128)S(1)}, f32[2,256]{1,0:T(2,128)}, u32[]{:S(2)}) copy-start(f32[2,256]{1,0:T(2,128)} %param.24) | copy-start | bytes 6148
  20.5 5.4 %copy-start.101 = (f32[2,256]{1,0:T(2,128)S(1)}, f32[2,256]{1,0:T(2,128)}, u32[]{:S(2)}) copy-start(f32[2,256]{1,0:T(2,128)} %param.27) | copy-start | bytes 6148
  21.0 112.1 %copy-start.6 = (f32[4,128,512]{2,1,0:T(8,128)}, f32[4,128,512]{2,1,0:T(8,128)S(1)}, u32[]{:S(2)}) copy-start(f32[4,128,512]{2,1,0:T(8,128)S(1)} %get-tuple-element.143) | copy-start | bytes 3145732
  21.3 17.5 %copy-start.83 = (f32[4,128]{1,0:T(4,128)}, f32[4,128]{1,0:T(4,128)S(1)}, u32[]{:S(2)}) copy-start(f32[4,128]{1,0:T(4,128)S(1)} %multiply_reduce_fusion.9) | copy-start | bytes 6148
  25.8 23.9 %copy-start.92 = (f32[1,256]{1,0:T(1,128)}, f32[1,256]{1,0:T(1,128)S(1)}, u32[]{:S(2)}) copy-start(f32[1,256]{1,0:T(1,128)S(1)} %get-tuple-element.135) | copy-start | bytes 3076
  25.8 23.9 %copy-start.94 = (f32[1,256]{1,0:T(1,128)}, f32[1,256]{1,0:T(1,128)S(1)}, u32[]{:S(2)}) copy-start(f32[1,256]{1,0:T(1,128)S(1)} %get-tuple-element.130) | copy-start | bytes 3076
  25.9 23.9 %copy-start.103 = (f32[1,256]{1,0:T(1,128)}, f32[1,256]{1,0:T(1,128)S(1)}, u32[]{:S(2)}) copy-start(f32[1,256]{1,0:T(1,128)S(1)} %get-tuple-element.133) | copy-start | bytes 3076
  25.9 23.8 %copy-start.105 = (f32[1,256]{1,0:T(1,128)}, f32[1,256]{1,0:T(1,128)S(1)}, u32[]{:S(2)}) copy-start(f32[1,256]{1,0:T(1,128)S(1)} %get-tuple-element.132) | copy-start | bytes 3076
  64.6 7.4 %copy-start.17 = (bf16[28,32,4,256]{3,1,2,0:T(8,128)(2,1)}, bf16[28,32,4,256]{3,1,2,0:T(8,128)(2,1)S(1)}, u32[]{:S(2)}) copy-start(bf16[28,32,4,256]{3,1,2,0:T(8,128)(2,1)S(1)} %get-tuple-element.96) | copy-start | bytes 5505028
  64.9 7.1 %copy-start.55 = (bf16[28,4,8,1,256]{4,2,1,3,0:T(8,128)(2,1)}, bf16[28,4,8,1,256]{4,2,1,3,0:T(8,128)(2,1)S(1)}, u32[]{:S(2)}) copy-start(bf16[28,4,8,1,256]{4,2,1,3,0:T(8,128)(2,1)S(1)} %pad.2) | copy-start | bytes 1376260
  65.0 7.0 %copy-start.57 = (bf16[28,4,8,1,256]{4,2,1,3,0:T(8,128)(2,1)}, bf16[28,4,8,1,256]{4,2,1,3,0:T(8,128)(2,1)S(1)}, u32[]{:S(2)}) copy-start(bf16[28,4,8,1,256]{4,2,1,3,0:T(8,128)(2,1)S(1)} %pad.3) | copy-start | bytes 1376260
  82.0 12.0 %copy-start.111 = (bf16[256,512]{1,0:T(8,128)(2,1)S(1)}, bf16[256,512]{1,0:T(8,128)(2,1)}, u32[]{:S(2)}) copy-start(bf16[256,512]{1,0:T(8,128)(2,1)} %param.28) | copy-start | bytes 786436
  82.0 12.0 %copy-start.113 = (f32[512]{0:T(512)S(1)}, f32[512]{0:T(512)}, u32[]{:S(2)}) copy-start(f32[512]{0:T(512)} %param.29) | copy-start | bytes 6148
  98.1 5.8 %copy-start.40 = (bf16[4,28,28,512]{3,0,2,1:T(4,128)(2,1)}, bf16[4,28,28,512]{3,0,2,1:T(4,128)(2,1)S(1)}, u32[]{:S(2)}) copy-start(bf16[4,28,28,512]{3,0,2,1:T(4,128)(2,1)S(1)} %copy.139) | copy-start | bytes 9633796
  123.3 4.7 copy-start.2
  128.0 5.2 %copy-start.33 = (bf16[2,512,512]{2,1,0:T(8,128)(2,1)S(1)}, bf16[2,512,512]{2,1,0:T(8,128)(2,1)}, u32[]{:S(2)}) copy-start(bf16[2,512,512]{2,1,0:T(8,128)(2,1)} %param.31) | copy-start | bytes 3145732
  135.5 5.1 copy-start.110
  135.5 5.1 copy-start.114
  150.8 16.1 %copy-start.8 = (f32[4,128,512]{2,1,0:T(8,128)}, f32[4,128,512]{2,1,0:T(8,128)S(1)}, u32[]{:S(2)}) copy-start(f32[4,128,512]{2,1,0:T(8,128)S(1)} %get-tuple-element.89) | copy-start | bytes 3145732
  152.9 14.1 %slice-start = ((s8[12845056]{0:T(1024)(128)(4,1)}), s8[4194304]{0:T(1024)(128)(4,1)S(1)}, s32[]{:S(2)}) async-start(s8[12845056]{0:T(1024)(128)(4,1)} %bitcast.377), calls=%async_computation.3 | async-start | bytes 8388608
  152.9 14.1 %slice-start.1 = ((s8[12845056]{0:T(1024)(128)(4,1)}), s8[4194304]{0:T(1024)(128)(4,1)S(1)}, s32[]{:S(2)}) async-start(s8[12845056]{0:T(1024)(128)(4,1)} %bitcast.377), calls=%async_computation.4 | async-start | bytes 8388608
  152.9 14.0 %slice-start.2 = ((s8[12845056]{0:T(1024)(128)(4,1)}), s8[4194304]{0:T(1024)(128)(4,1)S(1)}, s32[]{:S(2)}) async-start(s8[12845056]{0:T(1024)(128)(4,1)} %bitcast.377), calls=%async_computation.5 | async-start | bytes 8388608
  152.9 14.0 %slice-start.3 = ((s8[12845056]{0:T(1024)(128)(4,1)}), s8[262144]{0:T(1024)(128)(4,1)S(1)}, s32[]{:S(2)}) async-start(s8[12845056]{0:T(1024)(128)(4,1)} %bitcast.377), calls=%async_computation.6 | async-start | bytes 524288
  167.0 7.3 %copy-start.5 = (bf16[1,4,784,512]{2,3,1,0:T(8,128)(2,1)S(1)}, bf16[1,4,784,512]{2,3,1,0:T(8,128)(2,1)}, u32[]{:S(2)}) copy-start(bf16[1,4,784,512]{2,3,1,0:T(8,128)(2,1)} %copy.143) | copy-start | bytes 9633796
  175.8 51.2 %copy-start.53 = (bf16[4,8,64,128]{3,2,1,0:T(8,128)(2,1)}, bf16[4,8,64,128]{3,2,1,0:T(8,128)(2,1)S(1)}, u32[]{:S(2)}) copy-start(bf16[4,8,64,128]{3,2,1,0:T(8,128)(2,1)S(1)} %fusion.136) | copy-start | bytes 1572868
  187.4 7.0 %copy-start.10 = (bf16[28,4,32,256]{3,2,0,1:T(8,128)(2,1)S(1)}, bf16[28,4,32,256]{3,2,0,1:T(8,128)(2,1)}, u32[]{:S(2)}) copy-start(bf16[28,4,32,256]{3,2,0,1:T(8,128)(2,1)} %get-tuple-element.105) | copy-start | bytes 5505028
  208.1 9.9 %copy-start.35 = (f32[4,28,28,256]{3,2,1,0:T(8,128)S(1)}, f32[4,28,28,256]{3,2,1,0:T(8,128)}, u32[]{:S(2)}) copy-start(f32[4,28,28,256]{3,2,1,0:T(8,128)} %get-tuple-element.95) | copy-start | bytes 9633796
  225.1 4.2 copy-start.84
  229.4 5.3 %copy-start.4 = (f32[4,8,128,128]{2,3,1,0:T(8,128)S(1)}, f32[4,8,128,128]{2,3,1,0:T(8,128)}, u32[]{:S(2)}) copy-start(f32[4,8,128,128]{2,3,1,0:T(8,128)} %copy-done.3) | copy-start | bytes 6291460
  229.4 5.3 %copy-start.80 = (f32[4,8,128]{2,1,0:T(8,128)S(1)}, f32[4,8,128]{2,1,0:T(8,128)}, u32[]{:S(2)}) copy-start(f32[4,8,128]{2,1,0:T(8,128)} %log_add_fusion) | copy-start | bytes 49156
  236.6 5.5 %copy-start.54 = (bf16[4,8,64,128]{3,2,1,0:T(8,128)(2,1)S(1)}, bf16[4,8,64,128]{3,2,1,0:T(8,128)(2,1)}, u32[]{:S(2)}) copy-start(bf16[4,8,64,128]{3,2,1,0:T(8,128)(2,1)} %copy-done.53) | copy-start | bytes 1572868
  237.6 5.9 %copy-start.43 = (bf16[1,4,784,512]{3,2,0,1:T(8,128)(2,1)S(1)}, bf16[1,4,784,512]{3,2,0,1:T(8,128)(2,1)}, u32[]{:S(2)}) copy-start(bf16[1,4,784,512]{3,2,0,1:T(8,128)(2,1)} %copy.147) | copy-start | bytes 9633796
  238.8 4.7 copy-start.41
  238.8 4.7 copy-start.42
  243.5 4.8 copy-start.69
  243.5 4.8 copy-start.72
  243.5 6.5 %copy-start.39 = (bf16[4,784,512]{2,0,1:T(4,128)(2,1)S(1)}, bf16[4,784,512]{2,0,1:T(4,128)(2,1)}, u32[]{:S(2)}) copy-start(bf16[4,784,512]{2,0,1:T(4,128)(2,1)} %copy-done.38) | copy-start | bytes 9633796
  243.5 6.5 %copy-start.64 = (bf16[4,28,28,256]{3,2,1,0:T(8,128)(2,1)S(1)}, bf16[4,28,28,256]{3,2,1,0:T(8,128)(2,1)}, u32[]{:S(2)}) copy-start(bf16[4,28,28,256]{3,2,1,0:T(8,128)(2,1)} %copy-done.63) | copy-start | bytes 4816900
  255.1 4.0 copy-start.22
  271.3 4.9 copy-start.93
  271.3 4.9 copy-start.95
  271.3 4.9 copy-start.104
  271.3 4.9 copy-start.106
  271.3 4.9 copy-start.108
  293.0 5.1 copy-start.19
  293.0 5.1 copy-start.62
  343.4 7.7 %copy-start.82 = (f32[6144]{0:T(1024)S(1)}, f32[6144]{0:T(1024)}, u32[]{:S(2)}) copy-start(f32[6144]{0:T(1024)} %custom-call) | copy-start | bytes 73732
  343.4 7.7 %copy-start.102 = (f32[512]{0:T(512)S(1)}, f32[512]{0:T(512)}, u32[]{:S(2)}) copy-start(f32[512]{0:T(512)} %get-tuple-element.158) | copy-start | bytes 6148
  343.4 7.7 %copy-start.85 = (f32[512]{0:T(512)S(1)}, f32[512]{0:T(512)}, u32[]{:S(2)}) copy-start(f32[512]{0:T(512)} %convert_reduce_fusion.2) | copy-start | bytes 6148
  343.5 7.7 %copy-start.96 = (f32[512]{0:T(512)S(1)}, f32[512]{0:T(512)}, u32[]{:S(2)}) copy-start(f32[512]{0:T(512)} %get-tuple-element.77) | copy-start | bytes 6148
  343.5 7.8 %copy-start.91 = (f32[1024]{0:T(1024)S(1)}, f32[1024]{0:T(1024)}, u32[]{:S(2)}) copy-start(f32[1024]{0:T(1024)} %get-tuple-element.160) | copy-start | bytes 12292
  343.5 7.8 %copy-start.87 = (f32[512]{0:T(512)S(1)}, f32[512]{0:T(512)}, u32[]{:S(2)}) copy-start(f32[512]{0:T(512)} %get-tuple-element.84) | copy-start | bytes 6148
  343.5 68.9 %copy-start.16 = (f32[4,128,512]{2,1,0:T(8,128)S(1)}, f32[4,128,512]{2,1,0:T(8,128)}, u32[]{:S(2)}) copy-start(f32[4,128,512]{2,1,0:T(8,128)} %copy-done.15) | copy-start | bytes 3145732
  346.4 69.8 %all-to-all-start.1 = ((bf16[2,2,28,28,256]{4,1,3,0,2:T(2,128)(2,1)}), bf16[2,2,28,28,256]{4,1,3,0,2:T(2,128)(2,1)S(1)}, u32[]{:S(2)}, u32[]{:S(2)}) async-start(bf16[2,2,28,28,256]{4,1,3,0,2:T(2,128)(2,1)} %copy.153), calls=%async_computation.1 | async-start | bytes 3211264 | tf_op jit(solution)/shard_map/all_to_all | solution.py:317
  501.4 5.5 %copy-start.44 = (bf16[2,3,3,256,256]{4,3,2,1,0:T(8,128)(2,1)S(1)}, bf16[2,3,3,256,256]{4,3,2,1,0:T(8,128)(2,1)}, u32[]{:S(2)}) copy-start(bf16[2,3,3,256,256]{4,3,2,1,0:T(8,128)(2,1)} %get-tuple-element.79) | copy-start | bytes 7077892
  506.9 4.3 copy-start.66
  509.6 5.7 %copy-start.1 = (bf16[512,1024]{1,0:T(8,128)(2,1)S(1)}, bf16[512,1024]{1,0:T(8,128)(2,1)}, u32[]{:S(2)}) copy-start(bf16[512,1024]{1,0:T(8,128)(2,1)} %param.34) | copy-start | bytes 3145732
  (59 other events, 130.2 us)
Sparse Core Ops, SparseCore 0:
  308.9 192.4 all-reduce.2
